TPU v7x, 128 devices: a whole 4x4x4 slice. The times are simulated.
128 devices in a mesh: rep: 4 (over y_hi, core), fsdp: 32 (over x, z, y_lo).
Axes of the slice: x: 4, y: 4 (y_hi: 2, y_lo: 2; y = y_hi * 2 + y_lo), z: 4, core: 2. Of those that a mesh axis runs over, the one named last changes fastest.
Arguments:
- tokens: bfloat16 [98304, 4096], P(('rep', 'fsdp')), may hold values from -6 to 6
- cotangent: bfloat16 [98304, 1024], P(('rep', 'fsdp')), may hold values from -6 to 6
- weight: float32 [4096, 1024], P('fsdp'), may hold values from -0.09375 to 0.09375
- momentum: float32 [4, 4096, 1024], P('rep', 'fsdp'), may hold values from -6 to 6
- kept: int32 [4, 64, 16, 2], P(None, 'fsdp'), may hold values from 0 to 63, all different within a row
Outputs:
- input_grad: bfloat16 [98304, 4096], P(('rep', 'fsdp'))
- new_momentum: float32 [4, 4096, 1024], P('rep', 'fsdp')
- new_weight: float32 [4096, 1024], P('fsdp')
- update: float32 [4096, 1024], P('fsdp')
Inputs may be any that keep to these rules, and one draw needn't show every extreme that they name: `kept`: each row of the last dimension names 2 different block numbers.
All inputs are finite; a program needn't handle non-finite values.
Results may differ from a plain program's by a relative error of at most 0.0049.
Values may be sent and summed in bfloat16 or wider, within the bound.
A program may use at most 128 MiB of HBM per device.

v0:
```python
import jax
import jax.numpy as jnp
from jax import lax
from jax.sharding import PartitionSpec as P

TILE = 64
BLK = 8


decay_rate = 0.999
step_size = 0.02
highest = lax.Precision.HIGHEST


def dct_table():
    freq = jnp.arange(TILE, dtype=jnp.float32)[:, None]
    place = jnp.arange(TILE, dtype=jnp.float32)[None, :]
    table = jnp.cos(jnp.pi * (2.0 * place + 1.0) * freq / (2.0 * TILE))
    norms = jnp.where(freq == 0.0, jnp.sqrt(1.0 / TILE), jnp.sqrt(2.0 / TILE))
    return table * norms


def to_tiles(field):
    height, width = field.shape
    return field.reshape(height // TILE, TILE, width // TILE, TILE).transpose(0, 2, 1, 3)


def from_tiles(tiles):
    rows_t, cols_t = (tiles.shape[0], tiles.shape[1])
    return tiles.transpose(0, 2, 1, 3).reshape(rows_t * TILE, cols_t * TILE)


def forward_dct(tiles, table):
    return jnp.einsum("ij,abjk,lk->abil", table, tiles, table, precision=highest)


def inverse_dct(coefs, table):
    return jnp.einsum("ji,abjk,kl->abil", table, coefs, table, precision=highest)


def to_blocks(coefs):
    side = TILE // BLK
    rows_t, cols_t = (coefs.shape[0], coefs.shape[1])
    split = coefs.reshape(rows_t, cols_t, side, BLK, side, BLK).transpose(0, 1, 2, 4, 3, 5)
    return split.reshape(rows_t, cols_t, side * side, BLK * BLK)


def from_blocks(blocks):
    side = TILE // BLK
    rows_t, cols_t = (blocks.shape[0], blocks.shape[1])
    split = blocks.reshape(rows_t, cols_t, side, side, BLK, BLK).transpose(0, 1, 2, 4, 3, 5)
    return split.reshape(rows_t, cols_t, TILE, TILE)


def selector(kept):
    side = TILE // BLK
    return (kept[..., None] == jnp.arange(side * side, dtype=jnp.int32)).astype(jnp.float32)


def body(tokens, cotangent, weight, momentum, kept):
    table = dct_table()
    tok_count = tokens.shape[0]
    replicas = lax.axis_size("rep")
    shards = lax.axis_size("fsdp")
    weight_b = weight.astype(jnp.bfloat16)
    grad_wide = lax.dot_general(
        cotangent,
        lax.all_gather(weight_b, "fsdp", axis=0, tiled=True),
        (((1,), (1,)), ((), ())),
        preferred_element_type=jnp.float32,
    )
    input_grad = grad_wide.astype(jnp.bfloat16)
    summed = lax.psum_scatter(
        lax.dot_general(
            tokens, cotangent, (((0,), (0,)), ((), ())), preferred_element_type=jnp.float32
        ),
        "fsdp",
        scatter_dimension=0,
        tiled=True,
    )
    gradient = summed / jnp.sqrt(jnp.float32(tok_count * shards))
    current = decay_rate * momentum[0] + gradient
    coefs = forward_dct(to_tiles(current), table)
    own_kept = lax.dynamic_index_in_dim(kept, lax.axis_index("rep"), 0, keepdims=False)
    own_mask = selector(own_kept)
    compact = jnp.einsum("abkn,abnc->abkc", own_mask, to_blocks(coefs), precision=highest)
    own_dense = jnp.einsum("abkn,abkc->abnc", own_mask, compact, precision=highest)
    sent = from_tiles(inverse_dct(from_blocks(own_dense), table))
    new_momentum = (current - sent)[None]
    everyone = lax.all_gather(compact[None], "rep", axis=0, tiled=True)
    total = jnp.einsum("rabkn,rabkc->abnc", selector(kept), everyone, precision=highest)
    average = inverse_dct(from_blocks(total), table) / replicas
    spread = jnp.sqrt(jnp.mean(average * average, axis=(2, 3), keepdims=True) + 1e-06)
    update = from_tiles(average / (jnp.abs(average) + spread))
    new_weight = weight - step_size * update
    return (input_grad, new_momentum, new_weight, update)


def solution(mesh):
    in_specs = (
        P(("rep", "fsdp"), None),
        P(("rep", "fsdp"), None),
        P("fsdp", None),
        P("rep", "fsdp", None),
        P(None, "fsdp", None, None),
    )
    out_specs = (P(("rep", "fsdp"), None), P("rep", "fsdp", None), P("fsdp", None), P("fsdp", None))
    return jax.shard_map(body, mesh=mesh, in_specs=in_specs, out_specs=out_specs, check_vma=False)
```

profile of v0, /device:TPU:1, one launch (start us, length us, event | category | flops | bytes accessed | tf_op | source)
XLA Modules:
  0.0 642.6 jit_solution(12783955702759524694)
XLA Ops:
  7.2 1.4 copy-done
  8.6 13.0 %fusion.42 = f32[4096,1024]{1,0:T(8,128)} fusion(bf16[768,4096]{1,0:T(8,128)(2,1)} %param.5, bf16[768,1024]{1,0:T(8,128)(2,1)S(1)} %copy-done), kind=kOutput, calls=%fused_computation.59 | convolution fusion | flops 6442450944 | bytes 24641536 | tf_op jit(solution)/shard_map/dot_general | solution.py:74
  22.5 362.4 %reduce-scatter.2.cloned.1.call-done = f32[128,1024]{1,0:T(8,128)} async-done(((f32[4096,1024]{1,0:T(8,128)}), f32[128,1024]{1,0:T(8,128)}) %reduce-scatter.2.cloned.1.call-update) | async-done | bytes 524304 | tf_op jit(solution)/shard_map/reduce_scatter | solution.py:73
  384.9 1.1 bitcast_add_fusion
  386.3 1.4 copy.45
  387.8 4.4 fusion.1
  393.3 2.7 copy.47
  396.0 4.7 copy.48
  400.7 3.1 copy.49
  404.4 8.7 %all-gather = f32[8,16,2,64]{3,1,2,0:T(8,128)S(1)} all-gather(f32[2,16,2,64]{3,1,2,0:T(8,128)S(1)} %copy.56), channel_id=2, replica_groups=mesh['rep'=4,'fsdp'=32] {'rep'}, dimensions={0}, use_global_device_ids=true | all-gather | bytes 81920 | tf_op jit(solution)/shard_map/all_gather | solution.py:90
  413.1 1.1 convolution_bitcast_fusion
  414.2 2.7 copy.58
  417.0 4.7 copy.59
  421.7 4.0 copy.60
  425.7 3.2 fusion.6
  429.0 1.2 multiply_reduce_fusion
  432.2 2.5 multiply_subtract_fusion
  435.8 2.7 copy.50
  438.5 4.7 copy.51
  443.3 4.2 copy.52
  447.5 3.2 fusion.9
  453.6 1.9 subtract_bitcast_fusion
  455.5 168.3 %all-gather.3.cloned.1.call-done = bf16[4096,1024]{1,0:T(8,128)(2,1)} async-done(((bf16[128,1024]{1,0:T(8,128)(2,1)}), bf16[4096,1024]{1,0:T(8,128)(2,1)}) %all-gather.3.cloned.1.call-update) | async-done | bytes 8388624 | tf_op jit(solution)/shard_map/all_gather | solution.py:68
  623.8 12.0 %convolution_convert_fusion = bf16[768,4096]{1,0:T(8,128)(2,1)} fusion(bf16[768,1024]{1,0:T(8,128)(2,1)S(1)} %copy-done, bf16[4096,1024]{1,0:T(8,128)(2,1)} %all-gather.3.cloned.1.call-done), kind=kOutput, calls=%fused_computation | convolution fusion | flops 6445596672 | bytes 16252928 | tf_op jit(solution)/shard_map/dot_general | solution.py:66
  (25 shorter events, 8.9 us)
Async XLA Ops:
  7.2 1.4 copy-start
  7.2 377.8 %reduce-scatter.2.cloned.1.call-start = ((), (), s32[]{:S(2)}) async-start(), calls=%async_computation.2 | async-start | bytes 17301504 | tf_op jit(solution)/shard_map/reduce_scatter | solution.py:73
  21.6 0.7 copy-start.2
  21.6 363.3 %copy-start.1 = (f32[1,128,1024]{2,1,0:T(8,128)S(1)}, f32[1,128,1024]{2,1,0:T(8,128)}, u32[]{:S(2)}) copy-start(f32[1,128,1024]{2,1,0:T(8,128)} %param.8) | copy-start | bytes 1572868
  21.6 602.2 %all-gather.3.cloned.1.call-start = ((), (), s32[]{:S(2)}) async-start(), calls=%async_computation.1 | async-start | bytes 8650752 | tf_op jit(solution)/shard_map/all_gather | solution.py:68
Sparse Core Ops, SparseCore 0:
  21.7 363.1 reduce-scatter.1
  434.8 188.9 all-gather.2
where the time goes:
time: 644 us; the launch traced here: 643 us
  waiting for transfers between devices  531 us (82%)
  matrix products  42.1 us (7%)
  local copies, waits for them, and re-layouts  41 us (6%)
  between operations  14.1 us (2%)
  blocking collectives  8.69 us (1%)
    reduce_scatter x1, waiting for transfers between devices, body(): lax.psum_scatter(lax.dot_general(tokens, cotangent, (((0,), (0,)), ((), (...  362 us
    all_gather x1, waiting for transfers between devices, body(): lax.all_gather(weight_b, 'fsdp', axis=0, tiled=True)  168 us
    dot_general x1, matrix products, body(): lax.dot_general(tokens, cotangent, (((0,), (0,)), ((), ())), preferred_el...  13 us
  transfers between devices with their start and end apart: 2, of which 2 were waited for; matrix products, arithmetic and copies ran while one was open for 3% of the time, Pallas kernels for 0%

commit v1 on v0

v1 whole, which is shorter than its diff:
```python
import functools

import jax
import jax.numpy as jnp
import numpy as np
from jax import lax
from jax.experimental import pallas as pl
from jax.experimental.pallas import tpu as pltpu
from jax.sharding import PartitionSpec as P

TILE = 64
BLK = 8
DECAY = 0.999
STEP = 0.02
HIGHEST = lax.Precision.HIGHEST
MESH = pl.DeviceIdType.MESH
F32 = jnp.float32
BF16 = jnp.bfloat16

PIECES = (("yxz", 0, 256), ("yzx", 256, 128), ("xyz", 384, 256), ("zyx", 640, 384))
OFFS = (2, 1, 3, 0)


def dct_matrix():
    freq = np.arange(TILE, dtype=np.float64)[:, None]
    place = np.arange(TILE, dtype=np.float64)[None, :]
    table = np.cos(np.pi * (2.0 * place + 1.0) * freq / (2.0 * TILE))
    table *= np.where(freq == 0.0, np.sqrt(1.0 / TILE), np.sqrt(2.0 / TILE))
    return np.kron(np.eye(2), table).astype(np.float32)


def fold_matrix():
    fold = np.zeros((1024, 128), np.float32)
    lane = np.arange(1024)
    fold[lane, (lane // TILE) * BLK + lane % BLK] = 1.0
    return fold


def dot(a, b, dims=(((1,), (0,)), ((), ()))):
    return lax.dot_general(a, b, dims, precision=HIGHEST, preferred_element_type=F32)


def tile_transform(field, left, right):
    mid = dot(left, field)
    return jnp.concatenate([dot(mid[:, i * 128 : (i + 1) * 128], right) for i in range(8)], axis=1)


def kept_lanes(kept):
    tile_of = lax.broadcasted_iota(jnp.int32, (16, 1024), 1) // TILE
    here = tile_of == lax.broadcasted_iota(jnp.int32, (16, 1024), 0)
    found = []
    for which in range(2):
        rows = []
        for a in range(2):
            numbers = kept[a][:, which : which + 1]
            spread = jnp.where(here, jnp.broadcast_to(numbers, (16, 1024)), 0)
            rows.append(jnp.sum(spread, axis=0, keepdims=True))
        found.append(rows)
    return found


def kept_masks(kept):
    number = lax.broadcasted_iota(jnp.int32, (8, 8, 1024), 0) * 8 + (
        lax.broadcasted_iota(jnp.int32, (8, 8, 1024), 2) % TILE
    ) // BLK
    masks = []
    for rows in kept_lanes(kept):
        masks.append(
            [number == jnp.broadcast_to(row.reshape(1, 1, 1024), (8, 8, 1024)) for row in rows]
        )
    return masks


def make_places():
    rep, shard = lax.axis_index("rep"), lax.axis_index("fsdp")
    yhi, core = rep // 2, rep % 2
    x, z, ylo = shard // 8, (shard // 2) % 4, shard % 2

    def at(yhi_=None, core_=None, x_=None, z_=None, ylo_=None):
        h = yhi if yhi_ is None else yhi_
        c = core if core_ is None else core_
        xx = x if x_ is None else x_
        zz = z if z_ is None else z_
        l = ylo if ylo_ is None else ylo_
        return (h * 2 + c, (xx * 4 + zz) * 2 + l)

    return yhi, core, x, z, ylo, at


def main_kernel(
    tok_hbm, cot_hbm, w_hbm, mom_hbm, kept_ref, dct_ref, fold_ref,
    ig_hbm, newmom_ref, ex_ref,
    tok, cot, w, mom, wf, p0, p1, p2, p3, a0, a1, a2, a3, b0, b1, b2, b3, c0, c1, c2, c3,
    ig, cur, local_sem, ig_sem, send_sem, recv_sem,
):
    yhi, core, x, z, ylo, at = make_places()
    oy = 1 - ylo
    parts, r1, r2, r3 = (p0, p1, p2, p3), (a0, a1, a2, a3), (b0, b1, b2, b3), (c0, c1, c2, c3)
    xk = [lax.rem(x + o, 4) for o in OFFS]
    zo = [lax.rem(z + o, 4) for o in (2, 1, 3)]
    x_peer = [at(x_=xk[k]) for k in range(3)]
    z_peer = [at(z_=zo[i]) for i in range(3)]
    y_peer = at(ylo_=oy)
    y_far = at(yhi_=1 - yhi, ylo_=oy)
    core_peer = at(core_=1 - core)
    rep_peers = [core_peer, at(yhi_=1 - yhi), at(yhi_=1 - yhi, core_=1 - core)]

    w_load = pltpu.make_async_copy(w_hbm, w, local_sem.at[0])
    cot_load = pltpu.make_async_copy(cot_hbm, cot, local_sem.at[1])
    mom_load = pltpu.make_async_copy(mom_hbm.at[0], mom, local_sem.at[2])
    tok_loads = []
    for k in range(4):
        cols = pl.ds(pl.multiple_of(xk[k] * 1024, 1024), 1024)
        tok_loads.append(pltpu.make_async_copy(tok_hbm.at[:, cols], tok.at[:, cols], local_sem.at[3 + k]))
    w_load.start()
    cot_load.start()
    for load in tok_loads:
        load.start()
    mom_load.start()

    barrier = pltpu.get_barrier_semaphore()
    everyone = x_peer + z_peer + [y_peer, y_far] + rep_peers
    for peer in everyone:
        pl.semaphore_signal(barrier, inc=1, device_id=peer, device_id_type=MESH)

    used = [0]
    sent = []

    def send(src, dst, peer):
        n = used[0]
        used[0] += 1
        copy = pltpu.make_async_remote_copy(
            src_ref=src, dst_ref=dst, send_sem=send_sem.at[n], recv_sem=recv_sem.at[n],
            device_id=peer, device_id_type=MESH,
        )
        copy.start()
        sent.append(copy)
        return copy

    def same(view, peer):
        return send(view, view, peer)

    w_load.wait()
    half = pl.multiple_of(core * 64, 64)
    wf[x, z, ylo, pl.ds(half, 64)] = w[pl.ds(half, 64), :].astype(BF16)
    pl.semaphore_wait(barrier, len(everyone))
    rows_x, rows_z = pl.ds(half, 32), pl.ds(pl.multiple_of(half + 32, 32), 32)
    rows_c = pl.ds(half, 64)
    gx = [same(wf.at[x, z, ylo, rows_x], peer) for peer in x_peer]
    gz = [same(wf.at[x, z, ylo, rows_z], peer) for peer in z_peer]

    cot_load.wait()
    s1 = [[] for _ in PIECES]
    for k in range(4):
        xs = xk[k]
        tok_loads[k].wait()

        def block(zz, carry, xs=xs):
            cols = pl.ds(pl.multiple_of((xs * 4 + zz) * 256, 256), 256)
            part = lax.dot_general(
                tok[:, cols], cot[...], (((0,), (0,)), ((), ())), preferred_element_type=F32
            ).astype(BF16)
            for ref, (_, lo, width) in zip(parts, PIECES):
                ref[xs, zz, 0] = part[:128, lo : lo + width]
                ref[xs, zz, 1] = part[128:, lo : lo + width]
            return carry

        lax.fori_loop(0, 4, block, 0)
        for i, (order, _, _) in enumerate(PIECES):
            if order[0] == "y":
                s1[i].append(send(parts[i].at[xs, :, oy], r1[i].at[xs], y_peer))
            elif order[0] == "x":
                if k < 3:
                    s1[i].append(send(parts[i].at[xs], r1[i].at[k], x_peer[k]))
            else:
                s1[i].append(
                    [send(parts[i].at[xs, zo[j]], r1[i].at[xs, j], z_peer[j]) for j in range(3)]
                )
        if k == 1:
            for copy in gx + gz:
                copy.wait_recv()
            hx = [same(wf.at[:, z, ylo, rows_x], peer) for peer in z_peer]
            hz = [same(wf.at[x, :, ylo, rows_z], peer) for peer in x_peer]

    for copy in hx + hz:
        copy.wait_recv()
    far = same(wf.at[:, :, ylo, rows_c], y_far)
    near = same(wf.at[:, :, ylo, rows_c], core_peer)

    def add_into(ref, sources, count):
        def one(i, carry):
            total = ref(i)[...].astype(F32)
            for source in sources:
                total += source(i)[...].astype(F32)
            ref(i)[...] = total.astype(BF16)
            return carry

        lax.fori_loop(0, count, one, 0)

    def input_grad(plane, base):
        def one(i, carry):
            xx, zz = i // 2, (i % 2) * 2
            rows = jnp.concatenate([wf[xx, zz, plane], wf[xx, zz + 1, plane]], axis=0)
            out = lax.dot_general(
                cot[...], rows, (((1,), (1,)), ((), ())), preferred_element_type=F32
            ).astype(BF16)
            ig[base + i, 0] = out[:, :128]
            ig[base + i, 1] = out[:, 128:]
            for j in range(2):
                cols = pl.ds(pl.multiple_of(((xx * 4 + zz + j) * 2 + plane) * 128, 128), 128)
                pltpu.make_async_copy(ig.at[base + i, j], ig_hbm.at[:, cols], ig_sem.at[base + i, j]).start()
            return carry

        lax.fori_loop(0, 8, one, 0)

    near.wait_recv()
    input_grad(ylo, 0)

    s2 = [[] for _ in PIECES]
    for k in range(4):
        xs = xk[k]
        for i, (order, _, _) in enumerate(PIECES):
            if order[0] == "y":
                s1[i][k].wait_recv()
                add_into(
                    lambda c, i=i, xs=xs: parts[i].at[xs, c, ylo],
                    [lambda c, i=i, xs=xs: r1[i].at[xs, c]], 4,
                )
                if order == "yxz":
                    if k < 3:
                        s2[i].append(send(parts[i].at[xs, :, ylo], r2[i].at[k], x_peer[k]))
                else:
                    s2[i].append(
                        [send(parts[i].at[xs, zo[j], ylo], r2[i].at[xs, j], z_peer[j]) for j in range(3)]
                    )
            elif order == "zyx":
                for copy in s1[i][k]:
                    copy.wait_recv()
                add_into(
                    lambda c, i=i, xs=xs: parts[i].at[xs, z, c],
                    [lambda c, i=i, xs=xs, j=j: r1[i].at[xs, j, c] for j in range(3)], 2,
                )
                s2[i].append(send(parts[i].at[xs, z, oy], r2[i].at[xs], y_peer))
    for i, (order, _, _) in enumerate(PIECES):
        if order == "xyz":
            for copy in s1[i]:
                copy.wait_recv()
            add_into(
                lambda c, i=i: parts[i].at[x, c // 2, c % 2],
                [lambda c, i=i, j=j: r1[i].at[j, c // 2, c % 2] for j in range(3)], 8,
            )
            s2[i].append(send(parts[i].at[x, :, oy], r2[i].at[...], y_peer))

    s3 = [[] for _ in PIECES]
    for i, (order, _, _) in enumerate(PIECES):
        if order == "yxz" or order == "xyz":
            for copy in s2[i]:
                copy.wait_recv()
            if order == "yxz":
                sources = [lambda c, i=i, j=j: r2[i].at[j, c] for j in range(3)]
            else:
                sources = [lambda c, i=i: r2[i].at[c]]
            add_into(lambda c, i=i: parts[i].at[x, c, ylo], sources, 4)
            for j in range(3):
                s3[i].append(send(parts[i].at[x, zo[j], ylo], r3[i].at[j], z_peer[j]))
        else:
            for k in range(4):
                xs = xk[k]
                for copy in s2[i][k] if order == "yzx" else [s2[i][k]]:
                    copy.wait_recv()
                if order == "yzx":
                    sources = [lambda c, i=i, xs=xs, j=j: r2[i].at[xs, j] for j in range(3)]
                else:
                    sources = [lambda c, i=i, xs=xs: r2[i].at[xs]]
                add_into(lambda c, i=i, xs=xs: parts[i].at[xs, z, ylo], sources, 1)
                if k < 3:
                    s3[i].append(send(parts[i].at[xs, z, ylo], r3[i].at[k], x_peer[k]))

    far.wait_recv()
    near2 = same(wf.at[:, :, oy, rows_c], core_peer)
    near2.wait_recv()
    input_grad(oy, 8)

    mom_load.wait()
    for i, (_, lo, width) in enumerate(PIECES):
        for copy in s3[i]:
            copy.wait_recv()
        total = parts[i][x, z, ylo].astype(F32)
        for j in range(3):
            total += r3[i][j].astype(F32)
        cur[:, lo : lo + width] = DECAY * mom[:, lo : lo + width] + total * (1.0 / np.sqrt(24576.0))
    table = dct_ref[...]
    current = cur[...]
    coefs = tile_transform(current, table, table.T).reshape(2, 8, 8, 1024)
    me = lax.axis_index("rep")
    masks = kept_masks([kept_ref[me, a] for a in range(2)])
    folded, dense = [], []
    for which in range(2):
        for a in range(2):
            folded.append(jnp.sum(jnp.where(masks[which][a], coefs[a], 0.0), axis=0))
    for a in range(2):
        dense.append(jnp.where(masks[0][a] | masks[1][a], coefs[a], 0.0).reshape(64, 1024))
    ex_ref[me] = dot(jnp.concatenate(folded, axis=0), fold_ref[...])
    shared = [same(ex_ref.at[me], peer) for peer in rep_peers]
    newmom_ref[0] = current - tile_transform(jnp.concatenate(dense, axis=0), table.T, table)
    for copy in shared:
        copy.wait_recv()
    for copy in sent:
        copy.wait_send()

    def drain(i, carry):
        for j in range(2):
            pltpu.make_async_copy(ig.at[i, j], ig_hbm.at[:, pl.ds(0, 128)], ig_sem.at[i, j]).wait()
        return carry

    lax.fori_loop(0, 16, drain, 0)


def last_kernel(
    ig_in, mom_in, ex_ref, kept_ref, w_ref, dct_ref, fold_ref, ones_ref,
    ig_out, mom_out, neww_ref, upd_ref, sem,
):
    ig_copy = pltpu.make_async_copy(ig_in, ig_out, sem.at[0])
    mom_copy = pltpu.make_async_copy(mom_in, mom_out, sem.at[1])
    ig_copy.start()
    mom_copy.start()
    table = dct_ref[...]
    total = [jnp.zeros((8, 8, 1024), F32)] * 2
    spread_dims = (((1,), (1,)), ((), ()))
    wide = dot(ex_ref[...].reshape(128, 128), fold_ref[...], spread_dims).reshape(4, 2, 2, 8, 1024)
    for r in range(4):
        masks = kept_masks([kept_ref[r, a] for a in range(2)])
        for a in range(2):
            first = jnp.broadcast_to(wide[r, 0, a][None], (8, 8, 1024))
            second = jnp.broadcast_to(wide[r, 1, a][None], (8, 8, 1024))
            total[a] += jnp.where(masks[0][a], first, jnp.where(masks[1][a], second, 0.0))
    field = jnp.concatenate([t.reshape(64, 1024) for t in total], axis=0)
    average = tile_transform(field, table.T, table) * 0.25
    squares = jnp.sum((average * average).reshape(2, 64, 1024), axis=1)
    stacked = jnp.concatenate([squares[:, i * 128 : (i + 1) * 128] for i in range(8)], axis=0)
    means = dot(stacked, ones_ref[...]) * (1.0 / (TILE * TILE))
    spread = jnp.sqrt(means + 1e-06)
    for i in range(8):
        for a in range(2):
            rows, cols = slice(a * 64, a * 64 + 64), slice(i * 128, i * 128 + 128)
            avg = average[rows, cols]
            update = avg / (jnp.abs(avg) + spread[i * 2 + a : i * 2 + a + 1])
            upd_ref[rows, cols] = update
            neww_ref[rows, cols] = w_ref[rows, cols] - STEP * update
    ig_copy.wait()
    mom_copy.wait()


def body(tokens, cotangent, weight, momentum, kept):
    any_space = pl.BlockSpec(memory_space=pl.ANY)
    vmem = pl.BlockSpec(memory_space=pltpu.VMEM)
    first, second, third = [], [], []
    for order, _, width in PIECES:
        if order[0] == "y":
            first.append((4, 4, 128, width))
            second.append((3, 4, 128, width) if order == "yxz" else (4, 3, 128, width))
        elif order[0] == "x":
            first.append((3, 4, 2, 128, width))
            second.append((4, 128, width))
        else:
            first.append((4, 3, 2, 128, width))
            second.append((4, 128, width))
        third.append((3, 128, width))
    table, fold = jnp.asarray(dct_matrix()), jnp.asarray(fold_matrix())
    ones = jnp.asarray(np.kron(np.eye(2), np.ones((TILE, TILE))).astype(np.float32))
    sems = 96
    ig, newmom, shared = pl.pallas_call(
        main_kernel,
        out_shape=(
            jax.ShapeDtypeStruct((768, 4096), BF16),
            jax.ShapeDtypeStruct((1, 128, 1024), F32),
            jax.ShapeDtypeStruct((4, 32, 128), F32),
        ),
        in_specs=[any_space] * 4 + [vmem] * 3,
        out_specs=(any_space, vmem, vmem),
        scratch_shapes=[
            pltpu.VMEM((768, 4096), BF16),
            pltpu.VMEM((768, 1024), BF16),
            pltpu.VMEM((128, 1024), F32),
            pltpu.VMEM((128, 1024), F32),
            pltpu.VMEM((4, 4, 2, 128, 1024), BF16),
        ]
        + [pltpu.VMEM((4, 4, 2, 128, width), BF16) for _, _, width in PIECES]
        + [pltpu.VMEM(shape, BF16) for shape in first + second + third]
        + [
            pltpu.VMEM((16, 2, 768, 128), BF16),
            pltpu.VMEM((128, 1024), F32),
            pltpu.SemaphoreType.DMA((8,)),
            pltpu.SemaphoreType.DMA((16, 2)),
            pltpu.SemaphoreType.DMA((sems,)),
            pltpu.SemaphoreType.DMA((sems,)),
        ],
        compiler_params=pltpu.CompilerParams(
            collective_id=0, has_side_effects=True, vmem_limit_bytes=60 << 20
        ),
        cost_estimate=pl.CostEstimate(flops=13 * 10**9, bytes_accessed=20 * 10**6, transcendentals=0),
        name="gradients",
    )(tokens, cotangent, weight, momentum, kept, table, fold)
    return pl.pallas_call(
        last_kernel,
        out_shape=(
            jax.ShapeDtypeStruct((768, 4096), BF16),
            jax.ShapeDtypeStruct((1, 128, 1024), F32),
            jax.ShapeDtypeStruct((128, 1024), F32),
            jax.ShapeDtypeStruct((128, 1024), F32),
        ),
        in_specs=[any_space] * 2 + [vmem] * 6,
        out_specs=(any_space, any_space, vmem, vmem),
        scratch_shapes=[pltpu.SemaphoreType.DMA((2,))],
        compiler_params=pltpu.CompilerParams(vmem_limit_bytes=40 << 20),
        name="step",
    )(ig, newmom, shared, kept, weight, table, fold, ones)


def solution(mesh):
    in_specs = (
        P(("rep", "fsdp"), None),
        P(("rep", "fsdp"), None),
        P("fsdp", None),
        P("rep", "fsdp", None),
        P(None, "fsdp", None, None),
    )
    out_specs = (P(("rep", "fsdp"), None), P("rep", "fsdp", None), P("fsdp", None), P("fsdp", None))
    return jax.shard_map(body, mesh=mesh, in_specs=in_specs, out_specs=out_specs, check_vma=False)
```

time: 644 us -> 122 us (0.19)
  waiting for transfers between devices: 531 us -> 0 us
  Pallas kernels: 0 us -> 115 us
  matrix products: 42.1 us -> 0 us
  local copies, waits for them, and re-layouts: 41 us -> 6.12 us
  between operations: 14.1 us -> 0.7 us
  blocking collectives: 8.69 us -> 0 us
    reduce_scatter x1 -> x0, waiting for transfers between devices: 362 us -> none  [body(): lax.psum_scatter(lax.dot_general(tokens, cotangent, (((0,), (0,)), ((), (...]
    all_gather x1 -> x0, waiting for transfers between devices: 168 us -> none  [body(): lax.all_gather(weight_b, 'fsdp', axis=0, tiled=True)]
    pallas_call x0 -> x2, Pallas kernels: none -> 115 us  [the longest x1 111 us: body(): pl.pallas_call(main_kernel, out_shape=(jax.ShapeDtypeStruct((768, 4096),...]
    dot_general x11 -> x0, matrix products: 42.1 us -> none  [the longest x1 13 us: body(): lax.dot_general(tokens, cotangent, (((0,), (0,)), ((), ())), preferred_el...]
    reshape x7 -> x0, local copies, waits for them, and re-layouts: 15.2 us -> none  [the longest x2 8.27 us: from_blocks(): return split.reshape(rows_t, cols_t, TILE, TILE)]
    transpose x4 -> x0, local copies, waits for them, and re-layouts: 14.8 us -> none  [the longest x2 9.46 us: from_blocks(): blocks.reshape(rows_t, cols_t, side, side, BLK, BLK)]
    all_gather x1 -> x0, blocking collectives: 8.69 us -> none  [body(): everyone = lax.all_gather(compact[None], 'rep', axis=0, tiled=True)]
    dot_general x4 -> x0, local copies, waits for them, and re-layouts: 8.21 us -> none  [the longest x1 2.74 us: forward_dct(): jnp.einsum('ij,abjk,lk->abil', table, tiles, table, precision=highest)]
  transfers between devices with their start and end apart: 2 -> 0, of which waited for: 2 -> 0; matrix products, arithmetic and copies ran while one was open for 3% -> 0% of each run, Pallas kernels for 0% -> 0%
where the time goes in v1:
time: 122 us; the launch traced here: 121 us
  Pallas kernels  115 us (94%)
  local copies, waits for them, and re-layouts  6.12 us (5%)
    pallas_call x1, Pallas kernels, body(): pl.pallas_call(main_kernel, out_shape=(jax.ShapeDtypeStruct((768, 4096),...  111 us
    unnamed x17, local copies, waits for them, and re-layouts  6.12 us
    pallas_call x1, Pallas kernels, body(): pl.pallas_call(last_kernel, out_shape=(jax.ShapeDtypeStruct((768, 4096),...  3.86 us

profile of v1, /device:TPU:1, one launch (start us, length us, event | category | flops | bytes accessed | tf_op | source)
XLA Modules:
  0.0 121.5 jit_solution(4335267338559094556)
XLA Ops:
  0.6 1.4 %copy.12.kept_ref = s32[4,2,16,2]{3,2,1,0:T(8,128)} copy(s32[4,2,16,2]{2,3,1,0:T(2,128)} %param.12) | data formatting | bytes 2048 | tf_op args[4]
  2.1 0.0 copy-start.1
  2.1 0.0 copy-start.2
  2.1 0.0 copy-start.4
  2.1 0.0 copy-start.5
  2.1 0.0 copy-start.6
  2.1 110.8 %gradients.1 = (bf16[768,4096]{1,0:T(8,128)(2,1)}, f32[1,128,1024]{2,1,0:T(8,128)}, f32[4,32,128]{2,1,0:T(8,128)}) custom-call(bf16[768,4096]{1,0:T(8,128)(2,1)} %tok_hbm.1, bf16[768,1024]{1,0:T(8,128)(2,1)} %cot_hbm.1, f32[128,1024]{1,0:T(8,128)} %w_ref.1, f32[1,128,1024]{2,1,0:T(8,128)} %mom_hbm.1, s32[4,2,16,2]{3,2,1,0:T(8,128)} %copy.12.kept_ref, ...), custom_call_target="tpu_custom_call" | custom-call | flops 12999999488 | bytes 20000000 | tf_op jit(solution)/shard_map/gradients/pallas_call | solution.py:372
  112.9 0.0 copy-done.1
  112.9 0.0 copy-done.2
  112.9 0.0 copy-done.4
  112.9 0.0 copy-done.5
  112.9 0.0 copy-done.6
  113.0 0.0 copy-start
  113.0 2.8 %copy-done = bf16[768,4096]{1,0:T(8,128)(2,1)S(1)} copy-done((bf16[768,4096]{1,0:T(8,128)(2,1)S(1)}, bf16[768,4096]{1,0:T(8,128)(2,1)}, u32[]{:S(2)}) %copy-start) | copy-done | bytes 6291480
  115.7 0.0 copy-start.3
  115.7 1.0 copy-done.3
  116.8 0.0 copy-start.7
  116.8 0.8 copy-done.7
  117.6 3.9 %step.1 = (bf16[768,4096]{1,0:T(8,128)(2,1)}, f32[1,128,1024]{2,1,0:T(8,128)}, f32[128,1024]{1,0:T(8,128)}, f32[128,1024]{1,0:T(8,128)}) custom-call(bf16[768,4096]{1,0:T(8,128)(2,1)S(1)} %copy-done, f32[1,128,1024]{2,1,0:T(8,128)S(1)} %copy-done.3, f32[4,32,128]{2,1,0:T(8,128)S(1)} %copy-done.7, s32[4,2,16,2]{3,2,1,0:T(8,128)S(1)} %copy-done.4, ...), custom_call_target="tpu_custom_call" | custom-call | tf_op jit(solution)/shard_map/step/pallas_call | solution.py:404
Async XLA Ops:
  2.1 110.8 %copy-start.1 = (f32[128,1024]{1,0:T(8,128)S(1)}, f32[128,1024]{1,0:T(8,128)}, u32[]{:S(2)}) copy-start(f32[128,1024]{1,0:T(8,128)} %w_ref.1) | copy-start | bytes 1572868
  2.1 110.8 %copy-start.2 = (f32[1024,128]{1,0:T(8,128)S(1)}, f32[1024,128]{1,0:T(8,128)}, u32[]{:S(2)}) copy-start(f32[1024,128]{1,0:T(8,128)} %constant.7.clone.fold_ref) | copy-start | bytes 1572868
  2.1 110.8 %copy-start.4 = (s32[4,2,16,2]{3,2,1,0:T(8,128)S(1)}, s32[4,2,16,2]{3,2,1,0:T(8,128)}, u32[]{:S(2)}) copy-start(s32[4,2,16,2]{3,2,1,0:T(8,128)} %copy.12.kept_ref) | copy-start | bytes 3076
  2.1 110.9 %copy-start.5 = (f32[128,128]{1,0:T(8,128)S(1)}, f32[128,128]{1,0:T(8,128)}, u32[]{:S(2)}) copy-start(f32[128,128]{1,0:T(8,128)} %constant.6.clone.dct_ref) | copy-start | bytes 196612
  2.1 110.9 %copy-start.6 = (f32[128,128]{1,0:T(8,128)S(1)}, f32[128,128]{1,0:T(8,128)}, u32[]{:S(2)}) copy-start(f32[128,128]{1,0:T(8,128)} %constant.8.clone.ones_ref) | copy-start | bytes 196612
  113.0 2.8 %copy-start = (bf16[768,4096]{1,0:T(8,128)(2,1)S(1)}, bf16[768,4096]{1,0:T(8,128)(2,1)}, u32[]{:S(2)}) copy-start(bf16[768,4096]{1,0:T(8,128)(2,1)} %get-tuple-element.7.ig_in) | copy-start | bytes 18874372
  115.7 1.0 copy-start.3
  116.8 0.8 copy-start.7

commit v2 on v1

v2 whole, which is shorter than its diff:
```python
import jax
import jax.numpy as jnp
import numpy as np
from jax import lax
from jax.experimental import pallas as pl
from jax.experimental.pallas import tpu as pltpu
from jax.sharding import PartitionSpec as P

TILE = 64
BLK = 8
DECAY = 0.999
STEP = 0.02
MESH = pl.DeviceIdType.MESH
F32 = jnp.float32
BF16 = jnp.bfloat16

WIDTH = 128
Y_PIECES, X_PIECES, Z_PIECES = (0, 1), (2, 3, 4), (5, 6, 7)
OFFS = (2, 1, 3, 0)


def dct_matrix(copies):
    freq = np.arange(TILE, dtype=np.float64)[:, None]
    place = np.arange(TILE, dtype=np.float64)[None, :]
    table = np.cos(np.pi * (2.0 * place + 1.0) * freq / (2.0 * TILE))
    table *= np.where(freq == 0.0, np.sqrt(1.0 / TILE), np.sqrt(2.0 / TILE))
    return np.kron(np.eye(copies), table).astype(np.float32)


def two_halves(matrix):
    high = matrix.astype(jnp.bfloat16)
    low = (matrix - high.astype(np.float32)).astype(jnp.bfloat16)
    return np.stack([high, low])


def fold_matrix():
    fold = np.zeros((1024, 128), np.float32)
    lane = np.arange(1024)
    fold[lane, (lane // TILE) * BLK + lane % BLK] = 1.0
    return fold.astype(jnp.bfloat16)


def tile_lanes():
    return (np.arange(16)[:, None] == np.arange(1024)[None, :] // TILE).astype(jnp.bfloat16)


PLAIN = (((1,), (0,)), ((), ()))
TURNED = (((1,), (1,)), ((), ()))
FROM_LEFT = (((0,), (0,)), ((), ()))


def dot(a, b, dims=PLAIN):
    return lax.dot_general(a, b, dims, preferred_element_type=F32)


def halves(a):
    high = a.astype(BF16)
    return high, (a - high.astype(F32)).astype(BF16)


def dot_wide(a, b, dims=PLAIN):
    return dot(a[0], b[0], dims) + (dot(a[0], b[1], dims) + dot(a[1], b[0], dims))


def dot_exact(a, marks, dims=PLAIN):
    high, rest = a.astype(BF16), a
    rest = a - high.astype(F32)
    mid = rest.astype(BF16)
    low = (rest - mid.astype(F32)).astype(BF16)
    return dot(high, marks, dims) + (dot(mid, marks, dims) + dot(low, marks, dims))


def to_coefs(field, rows, lanes):
    mid = halves(dot_wide(rows, halves(field)))
    return jnp.concatenate(
        [dot_wide([m[:, i * 256 : i * 256 + 256] for m in mid], lanes, TURNED) for i in range(4)], axis=1
    )


def from_coefs(coefs, rows, lanes):
    mid = halves(dot_wide(rows, halves(coefs), FROM_LEFT))
    return jnp.concatenate(
        [dot_wide([m[:, i * 256 : i * 256 + 256] for m in mid], lanes) for i in range(4)], axis=1
    )


def kept_masks(kept, tile_lane):
    number = lax.broadcasted_iota(jnp.int32, (8, 8, 1024), 0) * 8 + (
        lax.broadcasted_iota(jnp.int32, (8, 8, 1024), 2) % TILE
    ) // BLK
    number = number.astype(F32)
    masks = [[], []]
    for rows in kept:
        spread = dot(rows.astype(F32).astype(BF16), tile_lane)
        for which in range(2):
            row = spread[which : which + 1].reshape(1, 1, 1024)
            masks[which].append(number == jnp.broadcast_to(row, (8, 8, 1024)))
    return masks


def make_places():
    rep, shard = lax.axis_index("rep"), lax.axis_index("fsdp")
    yhi, core = rep // 2, rep % 2
    x, z, ylo = shard // 8, (shard // 2) % 4, shard % 2

    def at(yhi_=None, core_=None, x_=None, z_=None, ylo_=None):
        h = yhi if yhi_ is None else yhi_
        c = core if core_ is None else core_
        xx = x if x_ is None else x_
        zz = z if z_ is None else z_
        l = ylo if ylo_ is None else ylo_
        return (h * 2 + c, (xx * 4 + zz) * 2 + l)

    return yhi, core, x, z, ylo, at


def main_kernel(
    tok_hbm, cot_hbm, w_hbm, mom_hbm, kept_hbm, rows_hbm, lanes_hbm, fold_hbm, tile_hbm,
    ig_hbm, newmom_hbm, ex_hbm,
    tok, cot, w, mom, kept_ref, rows_ref, lanes_ref, fold_ref, tile_ref,
    wf, parts, got_y, got_s1, got_x2, got_z2, got_y2, got_last,
    ig, cur, newmom, ex, local_sem, ig_sem, send_sem, recv_sem,
):
    yhi, core, x, z, ylo, at = make_places()
    oy = 1 - ylo
    xk = [lax.rem(x + o, 4) for o in OFFS]
    zk = [lax.rem(z + o, 4) for o in OFFS]
    x_peer = [at(x_=xk[k]) for k in range(3)]
    z_peer = [at(z_=zk[k]) for k in range(3)]
    y_peer = at(ylo_=oy)
    y_far = at(yhi_=1 - yhi, ylo_=oy)
    core_peer = at(core_=1 - core)
    rep_peers = [at(yhi_=1 - yhi), at(yhi_=1 - yhi, core_=1 - core), core_peer]

    w_load = pltpu.make_async_copy(w_hbm, w, local_sem.at[0])
    cot_load = pltpu.make_async_copy(cot_hbm, cot, local_sem.at[1])
    mom_load = pltpu.make_async_copy(mom_hbm.at[0], mom, local_sem.at[2])
    tok_loads = []
    for k in range(4):
        cols = pl.ds(pl.multiple_of(xk[k] * 1024, 1024), 1024)
        tok_loads.append(pltpu.make_async_copy(tok_hbm.at[:, cols], tok.at[:, cols], local_sem.at[3 + k]))
    w_load.start()
    cot_load.start()
    for load in tok_loads:
        load.start()
    mom_load.start()
    small = [(kept_hbm, kept_ref), (rows_hbm, rows_ref), (lanes_hbm, lanes_ref), (fold_hbm, fold_ref), (tile_hbm, tile_ref)]
    small = [pltpu.make_async_copy(src, dst, local_sem.at[7 + i]) for i, (src, dst) in enumerate(small)]
    for load in small:
        load.start()

    barrier = pltpu.get_barrier_semaphore()
    everyone = x_peer + z_peer + [y_peer, y_far] + rep_peers
    for peer in everyone:
        pl.semaphore_signal(barrier, inc=1, device_id=peer, device_id_type=MESH)

    used = [0]
    sent = []

    def send(src, dst, peer, tag="rs"):
        n = used[0]
        used[0] += 1
        copy = pltpu.make_async_remote_copy(
            src_ref=src, dst_ref=dst, send_sem=send_sem.at[n], recv_sem=recv_sem.at[n],
            device_id=peer, device_id_type=MESH,
        )
        copy.start()
        sent.append(copy)
        return copy

    def same(view, peer, tag="ag"):
        return send(view, view, peer, tag)

    w_load.wait()
    half = pl.multiple_of(core * 64, 64)
    rows_x, rows_z = pl.ds(half, 32), pl.ds(pl.multiple_of(half + 32, 32), 32)
    rows_c = pl.ds(half, 64)
    wf[x, z, ylo, rows_c] = w[rows_c, :].astype(BF16)
    pl.semaphore_wait(barrier, len(everyone))
    gx = [same(wf.at[x, z, ylo, rows_x], peer) for peer in x_peer]
    gz = [same(wf.at[x, z, ylo, rows_z], peer) for peer in z_peer]
    far = [(same(wf.at[x, z, ylo, rows_c], y_far, "far"), wf.at[x, z, oy, rows_c])]

    cot_load.wait()
    y1 = []
    for k in range(4):
        xs = xk[k]
        tok_loads[k].wait()

        def block(zz, carry, xs=xs):
            cols = pl.ds(pl.multiple_of((xs * 4 + zz) * 256, 256), 256)
            part = lax.dot_general(
                tok[:, cols], cot[...], FROM_LEFT, preferred_element_type=F32
            ).astype(BF16)
            for p in range(8):
                parts[p, xs, zz, 0] = part[:128, p * WIDTH : p * WIDTH + WIDTH]
                parts[p, xs, zz, 1] = part[128:, p * WIDTH : p * WIDTH + WIDTH]
            return carry

        lax.fori_loop(0, 4, block, 0)
        y1.append([send(parts.at[p, xs, :, oy], got_y.at[p, xs], y_peer) for p in Y_PIECES])
        if k == 0:
            for copy in gx + gz:
                copy.wait_recv()
            hx, hz = [None] * 3, [None] * 3
            for i in (1, 2, 0):
                hx[i] = same(wf.at[:, z, ylo, rows_x], z_peer[i])
                hz[i] = same(wf.at[x, :, ylo, rows_z], x_peer[i])
            for i in (1, 2, 0):
                far.append((same(wf.at[xk[i], z, ylo, rows_x], y_far, "far"), wf.at[xk[i], z, oy, rows_x]))
                far.append((same(wf.at[x, zk[i], ylo, rows_z], y_far, "far"), wf.at[x, zk[i], oy, rows_z]))

    def block_of(p, place, h):
        if p in X_PIECES:
            return parts.at[p, place, pl.ds(2 * h, 2)]
        return parts.at[p, pl.ds(2 * h, 2), place]

    def line(p):
        return (x, xk, x_peer) if p in X_PIECES else (z, zk, z_peer)

    s1 = {}

    def start_s1(p):
        _, places, peers = line(p)
        far_place, right, left = places[0], places[1], places[2]
        to_right, to_left = peers[1], peers[2]
        s1[p] = [
            send(block_of(p, far_place, 0), got_s1.at[p - 2, 0], to_right),
            send(block_of(p, far_place, 1), got_s1.at[p - 2, 1], to_left),
            send(block_of(p, right, 1), got_s1.at[p - 2, 2], to_right),
            send(block_of(p, left, 0), got_s1.at[p - 2, 3], to_left),
        ]

    def add_into(ref, sources, count):
        def one(i, carry):
            total = ref(i)[...].astype(F32)
            for source in sources:
                total += source(i)[...].astype(F32)
            ref(i)[...] = total.astype(BF16)
            return carry

        lax.fori_loop(0, count, one, 0)

    def chunk_of(p, place, h):
        if p in X_PIECES:
            return lambda c: parts.at[p, place, 2 * h + c // 2, c % 2]
        return lambda c: parts.at[p, 2 * h + c // 2, place, c % 2]

    def got(p, slot):
        return lambda c: got_s1.at[p - 2, slot, c // 2, c % 2]

    def pass_on(p):
        _, places, peers = line(p)
        right, left = places[1], places[2]
        s1[p][0].wait_recv()
        add_into(chunk_of(p, right, 0), [got(p, 0)], 4)
        s1[p].append(send(block_of(p, right, 0), got_s1.at[p - 2, 4], peers[1]))
        s1[p][1].wait_recv()
        add_into(chunk_of(p, left, 1), [got(p, 1)], 4)
        s1[p].append(send(block_of(p, left, 1), got_s1.at[p - 2, 5], peers[2]))

    def mine(p, c, y):
        if p in X_PIECES or p == Y_PIECES[0]:
            return parts.at[p, x, c, y]
        return parts.at[p, c, z, y]

    y2, last = {}, {}

    def finish_s1(p):
        place, _, _ = line(p)
        for copy in s1[p][2:]:
            copy.wait_recv()
        add_into(chunk_of(p, place, 0), [got(p, 3), got(p, 4)], 4)
        add_into(chunk_of(p, place, 1), [got(p, 2), got(p, 5)], 4)
        if p in X_PIECES:
            view = parts.at[p, x, :, oy]
        else:
            view = parts.at[p, :, z, oy]
        y2[p] = send(view, got_y2.at[p - 2], y_peer)

    def finish_y(p):
        y2[p].wait_recv()
        add_into(lambda c: mine(p, c, ylo), [lambda c: got_y2.at[p - 2, c]], 4)
        start_last(p)

    def start_last(p):
        peers, places = (z_peer, zk) if p in X_PIECES or p == Y_PIECES[0] else (x_peer, xk)
        last[p] = [send(mine(p, places[k], ylo), got_last.at[p, k], peers[k]) for k in range(3)]

    def input_grad(plane, base):
        def one(i, carry):
            xx, zz = i // 2, (i % 2) * 2
            rows = jnp.concatenate([wf[xx, zz, plane], wf[xx, zz + 1, plane]], axis=0)
            out = lax.dot_general(cot[...], rows, TURNED, preferred_element_type=F32).astype(BF16)
            ig[base + i, 0] = out[:, :128]
            ig[base + i, 1] = out[:, 128:]
            for j in range(2):
                cols = pl.ds(pl.multiple_of(((xx * 4 + zz + j) * 2 + plane) * 128, 128), 128)
                pltpu.make_async_copy(ig.at[base + i, j], ig_hbm.at[:, cols], ig_sem.at[base + i, j]).start()
            return carry

        lax.fori_loop(0, 8, one, 0)

    for p in (2, 5, 3, 6):
        start_s1(p)

    for i in (1, 2, 0):
        zs, xs = zk[(0, 2, 1)[i]], xk[(0, 2, 1)[i]]
        hx[i].wait_recv()
        far.append((same(wf.at[:, zs, ylo, rows_x], y_far, "far"), wf.at[:, zs, oy, rows_x]))
        hz[i].wait_recv()
        far.append((same(wf.at[xs, :, ylo, rows_z], y_far, "far"), wf.at[xs, :, oy, rows_z]))
    near = same(wf.at[:, :, ylo, rows_c], core_peer, "near")

    pass_on(2)
    pass_on(5)
    start_s1(4)
    start_s1(7)
    near.wait_recv()
    input_grad(ylo, 0)
    pass_on(3)
    pass_on(6)

    for k in range(4):
        xs = xk[k]
        for p in Y_PIECES:
            y1[k][p].wait_recv()
            add_into(
                lambda c, p=p, xs=xs: parts.at[p, xs, c, ylo], [lambda c, p=p, xs=xs: got_y.at[p, xs, c]], 4
            )
    x2 = [send(parts.at[0, xk[k], :, ylo], got_x2.at[k], x_peer[k]) for k in range(3)]
    z2 = [send(parts.at[1, :, zk[k], ylo], got_z2.at[k], z_peer[k]) for k in range(3)]
    pass_on(4)
    pass_on(7)
    finish_s1(2)
    finish_s1(5)

    def forward(count):
        for copy, view in far[:count]:
            copy.wait_recv()
            near2.append(same(view, core_peer, "far"))
        del far[:count]

    near2 = []
    forward(7)
    finish_s1(3)
    finish_s1(6)
    for copy in x2:
        copy.wait_recv()
    add_into(lambda c: mine(0, c, ylo), [lambda c, k=k: got_x2.at[k, c] for k in range(3)], 4)
    start_last(0)
    for copy in z2:
        copy.wait_recv()
    add_into(lambda c: mine(1, c, ylo), [lambda c, k=k: got_z2.at[k, c] for k in range(3)], 4)
    start_last(1)
    finish_y(2)
    finish_y(5)
    finish_s1(4)
    finish_s1(7)
    finish_y(3)
    finish_y(6)
    finish_y(4)
    finish_y(7)
    forward(6)

    mom_load.wait()
    for load in small:
        load.wait()
    for p in (0, 1, 2, 5, 3, 6, 4, 7):
        for copy in last[p]:
            copy.wait_recv()
        total = parts[p, x, z, ylo].astype(F32)
        for k in range(3):
            total += got_last[p, k].astype(F32)
        lo = p * WIDTH
        cur[:, lo : lo + WIDTH] = DECAY * mom[:, lo : lo + WIDTH] + total * (1.0 / np.sqrt(24576.0))
    rows, lanes = (rows_ref[0], rows_ref[1]), (lanes_ref[0], lanes_ref[1])
    coefs = to_coefs(cur[...], rows, lanes).reshape(2, 8, 8, 1024)
    me = lax.axis_index("rep")
    masks = kept_masks([kept_ref[me, a] for a in range(2)], tile_ref[...])
    folded, dense = [], []
    for which in range(2):
        for a in range(2):
            folded.append(jnp.sum(jnp.where(masks[which][a], coefs[a], 0.0), axis=0))
    ex[me] = dot_exact(jnp.concatenate(folded, axis=0), fold_ref[...])
    shared = [same(ex.at[me], peer, "ex") for peer in rep_peers]
    for a in range(2):
        dense.append(jnp.where(masks[0][a] | masks[1][a], coefs[a], 0.0).reshape(64, 1024))
    newmom[...] = cur[...] - from_coefs(jnp.concatenate(dense, axis=0), rows, lanes)
    newmom_store = pltpu.make_async_copy(newmom, newmom_hbm.at[0], local_sem.at[12])
    newmom_store.start()

    for copy in near2:
        copy.wait_recv()
    input_grad(oy, 8)
    for copy in shared:
        copy.wait_recv()
    ex_store = pltpu.make_async_copy(ex, ex_hbm, local_sem.at[13])
    ex_store.start()
    for copy in sent:
        copy.wait_send()

    def drain(i, carry):
        for j in range(2):
            pltpu.make_async_copy(ig.at[i, j], ig_hbm.at[:, pl.ds(0, 128)], ig_sem.at[i, j]).wait()
        return carry

    lax.fori_loop(0, 16, drain, 0)
    newmom_store.wait()
    ex_store.wait()


def last_kernel(
    ig_in, mom_in, ex_hbm, kept_hbm, w_hbm, rows_hbm, lanes_hbm, fold_hbm, tile_hbm, ones_hbm,
    ig_out, mom_out, neww_out, upd_out,
    ig, mom, ex_ref, w_ref, kept_ref, rows_ref, lanes_ref, fold_ref, tile_ref, ones_ref,
    neww_ref, upd_ref, sem,
):
    small = [
        (ex_hbm, ex_ref), (kept_hbm, kept_ref), (fold_hbm, fold_ref), (tile_hbm, tile_ref), (rows_hbm, rows_ref),
        (lanes_hbm, lanes_ref), (ones_hbm, ones_ref), (w_hbm, w_ref),
    ]
    small = [pltpu.make_async_copy(src, dst, sem.at[2, i]) for i, (src, dst) in enumerate(small)]
    for load in small:
        load.start()
    pieces = [(ig_in.at[pl.ds(i * 96, 96)], ig.at[pl.ds(i * 96, 96)], ig_out.at[pl.ds(i * 96, 96)]) for i in range(8)]
    pieces.append((mom_in, mom, mom_out))
    loads = [pltpu.make_async_copy(src, mid, sem.at[0, i]) for i, (src, mid, _) in enumerate(pieces)]
    stores = [pltpu.make_async_copy(mid, dst, sem.at[1, i]) for i, (_, mid, dst) in enumerate(pieces)]
    for load in loads:
        load.start()
    for load in small:
        load.wait()
    rows, lanes = (rows_ref[0], rows_ref[1]), (lanes_ref[0], lanes_ref[1])
    total = [jnp.zeros((8, 8, 1024), F32)] * 2
    wide = dot_exact(ex_ref[...].reshape(128, 128), fold_ref[...], TURNED).reshape(4, 2, 2, 8, 1024)
    for r in range(4):
        masks = kept_masks([kept_ref[r, a] for a in range(2)], tile_ref[...])
        for a in range(2):
            first = jnp.broadcast_to(wide[r, 0, a][None], (8, 8, 1024))
            second = jnp.broadcast_to(wide[r, 1, a][None], (8, 8, 1024))
            total[a] += jnp.where(masks[0][a], first, jnp.where(masks[1][a], second, 0.0))
    field = jnp.concatenate([t.reshape(64, 1024) for t in total], axis=0)
    for load, store in zip(loads, stores):
        load.wait()
        store.start()
    average = from_coefs(field, rows, lanes) * 0.25
    squares = jnp.sum((average * average).reshape(2, 64, 1024), axis=1)
    stacked = jnp.concatenate([squares[:, i * 128 : (i + 1) * 128] for i in range(8)], axis=0)
    means = dot_exact(stacked, ones_ref[...]) * (1.0 / (TILE * TILE))
    spread = jnp.sqrt(means + 1e-06)
    for i in range(8):
        for a in range(2):
            rows_a, cols = slice(a * 64, a * 64 + 64), slice(i * 128, i * 128 + 128)
            avg = average[rows_a, cols]
            update = avg / (jnp.abs(avg) + spread[i * 2 + a : i * 2 + a + 1])
            upd_ref[rows_a, cols] = update
            neww_ref[rows_a, cols] = w_ref[rows_a, cols] - STEP * update
    results = [(neww_ref, neww_out), (upd_ref, upd_out)]
    results = [pltpu.make_async_copy(src, dst, sem.at[1, 9 + i]) for i, (src, dst) in enumerate(results)]
    for store in results:
        store.start()
    for store in stores + results:
        store.wait()


def body(tokens, cotangent, weight, momentum, kept):
    any_space = pl.BlockSpec(memory_space=pl.ANY)
    rows, lanes = jnp.asarray(two_halves(dct_matrix(2))), jnp.asarray(two_halves(dct_matrix(4)))
    fold, tile_lane = jnp.asarray(fold_matrix()), jnp.asarray(tile_lanes())
    ones = jnp.asarray(np.kron(np.eye(2), np.ones((TILE, TILE))).astype(jnp.bfloat16))
    kept = kept.transpose(0, 1, 3, 2)
    constants = [
        pltpu.VMEM((4, 2, 2, 16), jnp.int32),
        pltpu.VMEM((2, 128, 128), BF16),
        pltpu.VMEM((2, 256, 256), BF16),
        pltpu.VMEM((1024, 128), BF16),
        pltpu.VMEM((16, 1024), BF16),
    ]
    sems = 160
    ig, newmom, shared = pl.pallas_call(
        main_kernel,
        out_shape=(
            jax.ShapeDtypeStruct((768, 4096), BF16),
            jax.ShapeDtypeStruct((1, 128, 1024), F32),
            jax.ShapeDtypeStruct((4, 32, 128), F32),
        ),
        in_specs=[any_space] * 9,
        out_specs=(any_space, any_space, any_space),
        scratch_shapes=[
            pltpu.VMEM((768, 4096), BF16),
            pltpu.VMEM((768, 1024), BF16),
            pltpu.VMEM((128, 1024), F32),
            pltpu.VMEM((128, 1024), F32),
            *constants,
            pltpu.VMEM((4, 4, 2, 128, 1024), BF16),
            pltpu.VMEM((8, 4, 4, 2, 128, WIDTH), BF16),
            pltpu.VMEM((2, 4, 4, 128, WIDTH), BF16),
            pltpu.VMEM((6, 6, 2, 2, 128, WIDTH), BF16),
            pltpu.VMEM((3, 4, 128, WIDTH), BF16),
            pltpu.VMEM((3, 4, 128, WIDTH), BF16),
            pltpu.VMEM((6, 4, 128, WIDTH), BF16),
            pltpu.VMEM((8, 3, 128, WIDTH), BF16),
            pltpu.VMEM((16, 2, 768, 128), BF16),
            pltpu.VMEM((128, 1024), F32),
            pltpu.VMEM((128, 1024), F32),
            pltpu.VMEM((4, 32, 128), F32),
            pltpu.SemaphoreType.DMA((14,)),
            pltpu.SemaphoreType.DMA((16, 2)),
            pltpu.SemaphoreType.DMA((sems,)),
            pltpu.SemaphoreType.DMA((sems,)),
        ],
        compiler_params=pltpu.CompilerParams(
            collective_id=0, has_side_effects=True, vmem_limit_bytes=60 << 20
        ),
        cost_estimate=pl.CostEstimate(flops=13 * 10**9, bytes_accessed=20 * 10**6, transcendentals=0),
        name="gradients",
    )(tokens, cotangent, weight, momentum, kept, rows, lanes, fold, tile_lane)
    return pl.pallas_call(
        last_kernel,
        out_shape=(
            jax.ShapeDtypeStruct((768, 4096), BF16),
            jax.ShapeDtypeStruct((1, 128, 1024), F32),
            jax.ShapeDtypeStruct((128, 1024), F32),
            jax.ShapeDtypeStruct((128, 1024), F32),
        ),
        in_specs=[any_space] * 10,
        out_specs=(any_space, any_space, any_space, any_space),
        scratch_shapes=[
            pltpu.VMEM((768, 4096), BF16),
            pltpu.VMEM((1, 128, 1024), F32),
            pltpu.VMEM((4, 32, 128), F32),
            pltpu.VMEM((128, 1024), F32),
            *constants,
            pltpu.VMEM((128, 128), BF16),
            pltpu.VMEM((128, 1024), F32),
            pltpu.VMEM((128, 1024), F32),
            pltpu.SemaphoreType.DMA((3, 12)),
        ],
        compiler_params=pltpu.CompilerParams(vmem_limit_bytes=60 << 20),
        name="step",
    )(ig, newmom, shared, kept, weight, rows, lanes, fold, tile_lane, ones)


def solution(mesh):
    in_specs = (
        P(("rep", "fsdp"), None),
        P(("rep", "fsdp"), None),
        P("fsdp", None),
        P("rep", "fsdp", None),
        P(None, "fsdp", None, None),
    )
    out_specs = (P(("rep", "fsdp"), None), P("rep", "fsdp", None), P("fsdp", None), P("fsdp", None))
    return jax.shard_map(body, mesh=mesh, in_specs=in_specs, out_specs=out_specs, check_vma=False)
```

time: 122 us -> 85.9 us (0.70)
  Pallas kernels: 115 us -> 84.8 us
  local copies, waits for them, and re-layouts: 6.12 us -> 0 us
    pallas_call x1, Pallas kernels: 111 us -> 78.4 us  [body(): pl.pallas_call(main_kernel, out_shape=(jax.ShapeDtypeStruct((768, 4096),...]
    unnamed x17 -> x0, local copies, waits for them, and re-layouts: 6.12 us -> none
    pallas_call x1, Pallas kernels: 3.86 us -> 6.49 us  [body(): pl.pallas_call(last_kernel, out_shape=(jax.ShapeDtypeStruct((768, 4096),...]
where the time goes in v2:
time: 85.9 us; the launch traced here: 85.5 us
  Pallas kernels  84.8 us (99%)
    pallas_call x1, Pallas kernels, body(): pl.pallas_call(main_kernel, out_shape=(jax.ShapeDtypeStruct((768, 4096),...  78.4 us
    pallas_call x1, Pallas kernels, body(): pl.pallas_call(last_kernel, out_shape=(jax.ShapeDtypeStruct((768, 4096),...  6.49 us

profile of v2, /device:TPU:1, one launch (start us, length us, event | category | flops | bytes accessed | tf_op | source)
XLA Modules:
  0.0 85.5 jit_solution(10712485226474645284)
XLA Ops:
  0.6 78.4 %gradients.1 = (bf16[768,4096]{1,0:T(8,128)(2,1)}, f32[1,128,1024]{2,1,0:T(8,128)}, f32[4,32,128]{2,1,0:T(8,128)}) custom-call(bf16[768,4096]{1,0:T(8,128)(2,1)} %tok_hbm.1, bf16[768,1024]{1,0:T(8,128)(2,1)} %cot_hbm.1, f32[128,1024]{1,0:T(8,128)} %w_hbm.3, f32[1,128,1024]{2,1,0:T(8,128)} %mom_hbm.1, s32[4,2,2,16]{3,2,1,0:T(2,128)} %bitcast.1, ...), custom_call_target="tpu_custom_call" | custom-call | flops 12999999488 | bytes 20000000 | tf_op jit(solution)/shard_map/gradients/pallas_call | solution.py:481
  79.0 6.5 %step.1 = (bf16[768,4096]{1,0:T(8,128)(2,1)}, f32[1,128,1024]{2,1,0:T(8,128)}, f32[128,1024]{1,0:T(8,128)}, f32[128,1024]{1,0:T(8,128)}) custom-call(bf16[768,4096]{1,0:T(8,128)(2,1)} %get-tuple-element.7.ig_in, f32[1,128,1024]{2,1,0:T(8,128)} %get-tuple-element.8.mom_in, f32[4,32,128]{2,1,0:T(8,128)} %get-tuple-element.9.ex_hbm, s32[4,2,2,16]{3,2,1,0:T(2,128)} %bitcast.2, ...), custom_call_target="tpu_custom_call" | custom-call | tf_op jit(solution)/shard_map/step/pallas_call | solution.py:519

commit v3 on v2

--- a/solution.py
+++ b/solution.py
@@ -40,10 +40,6 @@
     return fold.astype(jnp.bfloat16)
 
 
-def tile_lanes():
-    return (np.arange(16)[:, None] == np.arange(1024)[None, :] // TILE).astype(jnp.bfloat16)
-
-
 PLAIN = (((1,), (0,)), ((), ()))
 TURNED = (((1,), (1,)), ((), ()))
 FROM_LEFT = (((0,), (0,)), ((), ()))
@@ -58,44 +54,59 @@
     return high, (a - high.astype(F32)).astype(BF16)
 
 
-def dot_wide(a, b, dims=PLAIN):
-    return dot(a[0], b[0], dims) + (dot(a[0], b[1], dims) + dot(a[1], b[0], dims))
-
-
-def dot_exact(a, marks, dims=PLAIN):
-    high, rest = a.astype(BF16), a
+def dot_marks(a, marks, dims=PLAIN):
+    count = a.shape[0]
+    high = a.astype(BF16)
     rest = a - high.astype(F32)
     mid = rest.astype(BF16)
     low = (rest - mid.astype(F32)).astype(BF16)
-    return dot(high, marks, dims) + (dot(mid, marks, dims) + dot(low, marks, dims))
-
-
-def to_coefs(field, rows, lanes):
-    mid = halves(dot_wide(rows, halves(field)))
-    return jnp.concatenate(
-        [dot_wide([m[:, i * 256 : i * 256 + 256] for m in mid], lanes, TURNED) for i in range(4)], axis=1
-    )
-
-
-def from_coefs(coefs, rows, lanes):
-    mid = halves(dot_wide(rows, halves(coefs), FROM_LEFT))
-    return jnp.concatenate(
-        [dot_wide([m[:, i * 256 : i * 256 + 256] for m in mid], lanes) for i in range(4)], axis=1
-    )
-
-
-def kept_masks(kept, tile_lane):
-    number = lax.broadcasted_iota(jnp.int32, (8, 8, 1024), 0) * 8 + (
-        lax.broadcasted_iota(jnp.int32, (8, 8, 1024), 2) % TILE
+    out = dot(jnp.concatenate([high, mid, low], axis=0), marks, dims)
+    return out[:count] + (out[count : 2 * count] + out[2 * count :])
+
+
+def dot_left(table, field, dims=PLAIN):
+    high, low = halves(field)
+    if dims is FROM_LEFT:
+        return dot(table[0], high, dims) + (dot(table[0], low, dims) + dot(table[1], high, dims))
+    count = table.shape[1]
+    out = dot(table.reshape(2 * count, count), high, dims)
+    return out[:count] + (out[count:] + dot(table[0], low, dims))
+
+
+def dot_right(field, table, dims=PLAIN):
+    count = field.shape[0]
+    high, low = halves(field)
+    out = dot(jnp.concatenate([high, low], axis=0), table[0], dims)
+    return out[:count] + (out[count:] + dot(high, table[1], dims))
+
+
+def side_by_side(field, width):
+    return jnp.concatenate([field[:, i : i + width] for i in range(0, 1024, width)], axis=0)
+
+
+def from_coefs(coefs, rows):
+    count = coefs.shape[0]
+    none = jnp.zeros((128, 128), BF16)
+    lanes = [
+        jnp.concatenate([jnp.concatenate([r, none], axis=1), jnp.concatenate([none, r], axis=1)], axis=0)
+        for r in (rows[0], rows[1])
+    ]
+    mid = side_by_side(dot_left(rows, coefs, FROM_LEFT), 256)
+    out = dot_right(mid, lanes)
+    return jnp.concatenate([out[i * count : i * count + count] for i in range(4)], axis=1)
+
+
+def block_numbers(width):
+    number = lax.broadcasted_iota(jnp.int32, (8, 8, width), 0) * 8 + (
+        lax.broadcasted_iota(jnp.int32, (8, 8, width), 2) % TILE
     ) // BLK
-    number = number.astype(F32)
-    masks = [[], []]
-    for rows in kept:
-        spread = dot(rows.astype(F32).astype(BF16), tile_lane)
-        for which in range(2):
-            row = spread[which : which + 1].reshape(1, 1, 1024)
-            masks[which].append(number == jnp.broadcast_to(row, (8, 8, 1024)))
-    return masks
+    return number.astype(F32)
+
+
+def kept_lanes(kept):
+    tile = lax.broadcasted_iota(jnp.int32, (16, 1024), 0)
+    marks = jnp.where(tile == lax.broadcasted_iota(jnp.int32, (16, 1024), 1) // TILE, 1.0, 0.0)
+    return dot(kept.astype(F32).astype(BF16), marks.astype(BF16))
 
 
 def make_places():
@@ -115,11 +126,11 @@
 
 
 def main_kernel(
-    tok_hbm, cot_hbm, w_hbm, mom_hbm, kept_hbm, rows_hbm, lanes_hbm, fold_hbm, tile_hbm,
+    tok_hbm, cot_hbm, w_hbm, mom_hbm, kept_hbm, rows_hbm, fold_hbm,
     ig_hbm, newmom_hbm, ex_hbm,
-    tok, cot, w, mom, kept_ref, rows_ref, lanes_ref, fold_ref, tile_ref,
+    tok, cot, w, mom, kept_ref, rows_ref, fold_ref,
     wf, parts, got_y, got_s1, got_x2, got_z2, got_y2, got_last,
-    ig, cur, newmom, ex, local_sem, ig_sem, send_sem, recv_sem,
+    ig, cur, newmom, dense, numbers, ex, local_sem, ig_sem, send_sem, recv_sem,
 ):
     yhi, core, x, z, ylo, at = make_places()
     oy = 1 - ylo
@@ -132,7 +143,8 @@
     core_peer = at(core_=1 - core)
     rep_peers = [at(yhi_=1 - yhi), at(yhi_=1 - yhi, core_=1 - core), core_peer]
 
-    w_load = pltpu.make_async_copy(w_hbm, w, local_sem.at[0])
+    half = pl.multiple_of(core * 64, 64)
+    w_load = pltpu.make_async_copy(w_hbm.at[pl.ds(half, 64)], w, local_sem.at[0])
     cot_load = pltpu.make_async_copy(cot_hbm, cot, local_sem.at[1])
     mom_load = pltpu.make_async_copy(mom_hbm.at[0], mom, local_sem.at[2])
     tok_loads = []
@@ -144,7 +156,7 @@
     for load in tok_loads:
         load.start()
     mom_load.start()
-    small = [(kept_hbm, kept_ref), (rows_hbm, rows_ref), (lanes_hbm, lanes_ref), (fold_hbm, fold_ref), (tile_hbm, tile_ref)]
+    small = [(kept_hbm, kept_ref), (rows_hbm, rows_ref), (fold_hbm, fold_ref)]
     small = [pltpu.make_async_copy(src, dst, local_sem.at[7 + i]) for i, (src, dst) in enumerate(small)]
     for load in small:
         load.start()
@@ -172,10 +184,9 @@
         return send(view, view, peer, tag)
 
     w_load.wait()
-    half = pl.multiple_of(core * 64, 64)
     rows_x, rows_z = pl.ds(half, 32), pl.ds(pl.multiple_of(half + 32, 32), 32)
     rows_c = pl.ds(half, 64)
-    wf[x, z, ylo, rows_c] = w[rows_c, :].astype(BF16)
+    wf[x, z, ylo, rows_c] = w[...].astype(BF16)
     pl.semaphore_wait(barrier, len(everyone))
     gx = [same(wf.at[x, z, ylo, rows_x], peer) for peer in x_peer]
     gz = [same(wf.at[x, z, ylo, rows_z], peer) for peer in z_peer]
@@ -203,7 +214,7 @@
             for copy in gx + gz:
                 copy.wait_recv()
             hx, hz = [None] * 3, [None] * 3
-            for i in (1, 2, 0):
+            for i in (1, 2):
                 hx[i] = same(wf.at[:, z, ylo, rows_x], z_peer[i])
                 hz[i] = same(wf.at[x, :, ylo, rows_z], x_peer[i])
             for i in (1, 2, 0):
@@ -287,7 +298,43 @@
         peers, places = (z_peer, zk) if p in X_PIECES or p == Y_PIECES[0] else (x_peer, xk)
         last[p] = [send(mine(p, places[k], ylo), got_last.at[p, k], peers[k]) for k in range(3)]
 
-    def input_grad(plane, base):
+    me = lax.axis_index("rep")
+
+    def prepare():
+        mom_load.wait()
+        for load in small:
+            load.wait()
+        numbers[...] = kept_lanes(kept_ref[me])
+        ex[me] = jnp.zeros((32, 128), F32)
+
+    def finish(p):
+        for copy in last[p]:
+            copy.wait_recv()
+        total = parts[p, x, z, ylo].astype(F32)
+        for k in range(3):
+            total += got_last[p, k].astype(F32)
+        cols = slice(p * WIDTH, p * WIDTH + WIDTH)
+        current = DECAY * mom[:, cols] + total * (1.0 / np.sqrt(24576.0))
+        cur[:, cols] = current
+        mid = dot_left(rows_ref[...], current)
+        coefs = dot_right(mid, rows_ref[...], TURNED).reshape(2, 8, 8, WIDTH)
+        places = block_numbers(WIDTH)
+        masks = [
+            [
+                places == jnp.broadcast_to(numbers[2 * a + which, cols].reshape(1, 1, WIDTH), (8, 8, WIDTH))
+                for a in range(2)
+            ]
+            for which in range(2)
+        ]
+        folded = [
+            jnp.sum(jnp.where(masks[which][a], coefs[a], 0.0), axis=0) for which in range(2) for a in range(2)
+        ]
+        ex[me] += dot_marks(jnp.concatenate(folded, axis=0), fold_ref[cols])
+        for a in range(2):
+            kept_here = jnp.where(masks[0][a] | masks[1][a], coefs[a], 0.0)
+            dense[a * 64 : a * 64 + 64, cols] = kept_here.reshape(64, WIDTH)
+
+    def input_grad(plane, base, low, high):
         def one(i, carry):
             xx, zz = i // 2, (i % 2) * 2
             rows = jnp.concatenate([wf[xx, zz, plane], wf[xx, zz + 1, plane]], axis=0)
@@ -299,28 +346,35 @@
                 pltpu.make_async_copy(ig.at[base + i, j], ig_hbm.at[:, cols], ig_sem.at[base + i, j]).start()
             return carry
 
-        lax.fori_loop(0, 8, one, 0)
-
+        lax.fori_loop(low, high, one, 0)
+
+    onward = []
+    for i in (1, 2):
+        zs, xs = zk[3 - i], xk[3 - i]
+        pair = pl.ds(2 * (i - 1), 2)
+        hx[i].wait_recv()
+        onward.append(same(wf.at[pair, zs, ylo, rows_x], z_peer[i]))
+        far.append((same(wf.at[:, zs, ylo, rows_x], y_far, "far"), wf.at[:, zs, oy, rows_x]))
+        hz[i].wait_recv()
+        onward.append(same(wf.at[xs, pair, ylo, rows_z], x_peer[i]))
+        far.append((same(wf.at[xs, :, ylo, rows_z], y_far, "far"), wf.at[xs, :, oy, rows_z]))
     for p in (2, 5, 3, 6):
         start_s1(p)
-
-    for i in (1, 2, 0):
-        zs, xs = zk[(0, 2, 1)[i]], xk[(0, 2, 1)[i]]
-        hx[i].wait_recv()
-        far.append((same(wf.at[:, zs, ylo, rows_x], y_far, "far"), wf.at[:, zs, oy, rows_x]))
-        hz[i].wait_recv()
-        far.append((same(wf.at[xs, :, ylo, rows_z], y_far, "far"), wf.at[xs, :, oy, rows_z]))
-    near = same(wf.at[:, :, ylo, rows_c], core_peer, "near")
-
     pass_on(2)
     pass_on(5)
     start_s1(4)
     start_s1(7)
+    for copy in onward:
+        copy.wait_recv()
+    far.append((same(wf.at[:, zk[0], ylo, rows_x], y_far, "far"), wf.at[:, zk[0], oy, rows_x]))
+    far.append((same(wf.at[xk[0], :, ylo, rows_z], y_peer, "far"), wf.at[xk[0], :, oy, rows_z]))
+    near = same(wf.at[:, :, ylo, rows_c], core_peer, "near")
     near.wait_recv()
-    input_grad(ylo, 0)
+    input_grad(ylo, 0, 0, 8)
     pass_on(3)
     pass_on(6)
 
+    prepare()
     for k in range(4):
         xs = xk[k]
         for p in Y_PIECES:
@@ -328,10 +382,10 @@
             add_into(
                 lambda c, p=p, xs=xs: parts.at[p, xs, c, ylo], [lambda c, p=p, xs=xs: got_y.at[p, xs, c]], 4
             )
+    pass_on(4)
+    pass_on(7)
     x2 = [send(parts.at[0, xk[k], :, ylo], got_x2.at[k], x_peer[k]) for k in range(3)]
     z2 = [send(parts.at[1, :, zk[k], ylo], got_z2.at[k], z_peer[k]) for k in range(3)]
-    pass_on(4)
-    pass_on(7)
     finish_s1(2)
     finish_s1(5)
 
@@ -345,6 +399,10 @@
     forward(7)
     finish_s1(3)
     finish_s1(6)
+    finish_y(2)
+    finish_y(5)
+    finish_s1(4)
+    finish_s1(7)
     for copy in x2:
         copy.wait_recv()
     add_into(lambda c: mine(0, c, ylo), [lambda c, k=k: got_x2.at[k, c] for k in range(3)], 4)
@@ -353,46 +411,28 @@
         copy.wait_recv()
     add_into(lambda c: mine(1, c, ylo), [lambda c, k=k: got_z2.at[k, c] for k in range(3)], 4)
     start_last(1)
-    finish_y(2)
-    finish_y(5)
-    finish_s1(4)
-    finish_s1(7)
     finish_y(3)
     finish_y(6)
+    forward(6)
+    finish(2)
+    finish(5)
     finish_y(4)
     finish_y(7)
-    forward(6)
-
-    mom_load.wait()
-    for load in small:
-        load.wait()
-    for p in (0, 1, 2, 5, 3, 6, 4, 7):
-        for copy in last[p]:
-            copy.wait_recv()
-        total = parts[p, x, z, ylo].astype(F32)
-        for k in range(3):
-            total += got_last[p, k].astype(F32)
-        lo = p * WIDTH
-        cur[:, lo : lo + WIDTH] = DECAY * mom[:, lo : lo + WIDTH] + total * (1.0 / np.sqrt(24576.0))
-    rows, lanes = (rows_ref[0], rows_ref[1]), (lanes_ref[0], lanes_ref[1])
-    coefs = to_coefs(cur[...], rows, lanes).reshape(2, 8, 8, 1024)
-    me = lax.axis_index("rep")
-    masks = kept_masks([kept_ref[me, a] for a in range(2)], tile_ref[...])
-    folded, dense = [], []
-    for which in range(2):
-        for a in range(2):
-            folded.append(jnp.sum(jnp.where(masks[which][a], coefs[a], 0.0), axis=0))
-    ex[me] = dot_exact(jnp.concatenate(folded, axis=0), fold_ref[...])
+    for copy in near2:
+        copy.wait_recv()
+    input_grad(oy, 8, 0, 4)
+    finish(3)
+    finish(6)
+    finish(0)
+    finish(1)
+    finish(4)
+    finish(7)
     shared = [same(ex.at[me], peer, "ex") for peer in rep_peers]
-    for a in range(2):
-        dense.append(jnp.where(masks[0][a] | masks[1][a], coefs[a], 0.0).reshape(64, 1024))
-    newmom[...] = cur[...] - from_coefs(jnp.concatenate(dense, axis=0), rows, lanes)
+    newmom[...] = cur[...] - from_coefs(dense[...], rows_ref[...])
     newmom_store = pltpu.make_async_copy(newmom, newmom_hbm.at[0], local_sem.at[12])
     newmom_store.start()
 
-    for copy in near2:
-        copy.wait_recv()
-    input_grad(oy, 8)
+    input_grad(oy, 8, 4, 8)
     for copy in shared:
         copy.wait_recv()
     ex_store = pltpu.make_async_copy(ex, ex_hbm, local_sem.at[13])
@@ -411,14 +451,14 @@
 
 
 def last_kernel(
-    ig_in, mom_in, ex_hbm, kept_hbm, w_hbm, rows_hbm, lanes_hbm, fold_hbm, tile_hbm, ones_hbm,
+    ig_in, mom_in, ex_hbm, kept_hbm, w_hbm, rows_hbm, fold_hbm, ones_hbm,
     ig_out, mom_out, neww_out, upd_out,
-    ig, mom, ex_ref, w_ref, kept_ref, rows_ref, lanes_ref, fold_ref, tile_ref, ones_ref,
+    ig, mom, ex_ref, w_ref, kept_ref, rows_ref, fold_ref, ones_ref,
     neww_ref, upd_ref, sem,
 ):
     small = [
-        (ex_hbm, ex_ref), (kept_hbm, kept_ref), (fold_hbm, fold_ref), (tile_hbm, tile_ref), (rows_hbm, rows_ref),
-        (lanes_hbm, lanes_ref), (ones_hbm, ones_ref), (w_hbm, w_ref),
+        (ex_hbm, ex_ref), (kept_hbm, kept_ref), (fold_hbm, fold_ref), (rows_hbm, rows_ref), (ones_hbm, ones_ref),
+        (w_hbm, w_ref),
     ]
     small = [pltpu.make_async_copy(src, dst, sem.at[2, i]) for i, (src, dst) in enumerate(small)]
     for load in small:
@@ -431,23 +471,25 @@
         load.start()
     for load in small:
         load.wait()
-    rows, lanes = (rows_ref[0], rows_ref[1]), (lanes_ref[0], lanes_ref[1])
     total = [jnp.zeros((8, 8, 1024), F32)] * 2
-    wide = dot_exact(ex_ref[...].reshape(128, 128), fold_ref[...], TURNED).reshape(4, 2, 2, 8, 1024)
+    wide = dot_marks(ex_ref[...].reshape(128, 128), fold_ref[...], TURNED).reshape(4, 2, 2, 8, 1024)
+    numbers = kept_lanes(kept_ref[...].reshape(16, 16))
+    places = block_numbers(1024)
     for r in range(4):
-        masks = kept_masks([kept_ref[r, a] for a in range(2)], tile_ref[...])
         for a in range(2):
-            first = jnp.broadcast_to(wide[r, 0, a][None], (8, 8, 1024))
-            second = jnp.broadcast_to(wide[r, 1, a][None], (8, 8, 1024))
-            total[a] += jnp.where(masks[0][a], first, jnp.where(masks[1][a], second, 0.0))
+            value = 0.0
+            for which in (1, 0):
+                at = r * 4 + a * 2 + which
+                mask = places == jnp.broadcast_to(numbers[at : at + 1].reshape(1, 1, 1024), (8, 8, 1024))
+                value = jnp.where(mask, jnp.broadcast_to(wide[r, which, a][None], (8, 8, 1024)), value)
+            total[a] += value
+        for load, store in list(zip(loads, stores))[2 * r : 2 * r + 2 + r // 3]:
+            load.wait()
+            store.start()
     field = jnp.concatenate([t.reshape(64, 1024) for t in total], axis=0)
-    for load, store in zip(loads, stores):
-        load.wait()
-        store.start()
-    average = from_coefs(field, rows, lanes) * 0.25
+    average = from_coefs(field, rows_ref[...]) * 0.25
     squares = jnp.sum((average * average).reshape(2, 64, 1024), axis=1)
-    stacked = jnp.concatenate([squares[:, i * 128 : (i + 1) * 128] for i in range(8)], axis=0)
-    means = dot_exact(stacked, ones_ref[...]) * (1.0 / (TILE * TILE))
+    means = dot_marks(side_by_side(squares, 128), ones_ref[...]) * (1.0 / (TILE * TILE))
     spread = jnp.sqrt(means + 1e-06)
     for i in range(8):
         for a in range(2):
@@ -466,16 +508,13 @@
 
 def body(tokens, cotangent, weight, momentum, kept):
     any_space = pl.BlockSpec(memory_space=pl.ANY)
-    rows, lanes = jnp.asarray(two_halves(dct_matrix(2))), jnp.asarray(two_halves(dct_matrix(4)))
-    fold, tile_lane = jnp.asarray(fold_matrix()), jnp.asarray(tile_lanes())
+    rows, fold = jnp.asarray(two_halves(dct_matrix(2))), jnp.asarray(fold_matrix())
     ones = jnp.asarray(np.kron(np.eye(2), np.ones((TILE, TILE))).astype(jnp.bfloat16))
-    kept = kept.transpose(0, 1, 3, 2)
+    kept = kept.transpose(0, 1, 3, 2).reshape(4, 4, 16)
     constants = [
-        pltpu.VMEM((4, 2, 2, 16), jnp.int32),
+        pltpu.VMEM((4, 4, 16), jnp.int32),
         pltpu.VMEM((2, 128, 128), BF16),
-        pltpu.VMEM((2, 256, 256), BF16),
         pltpu.VMEM((1024, 128), BF16),
-        pltpu.VMEM((16, 1024), BF16),
     ]
     sems = 160
     ig, newmom, shared = pl.pallas_call(
@@ -485,12 +524,12 @@
             jax.ShapeDtypeStruct((1, 128, 1024), F32),
             jax.ShapeDtypeStruct((4, 32, 128), F32),
         ),
-        in_specs=[any_space] * 9,
+        in_specs=[any_space] * 7,
         out_specs=(any_space, any_space, any_space),
         scratch_shapes=[
             pltpu.VMEM((768, 4096), BF16),
             pltpu.VMEM((768, 1024), BF16),
-            pltpu.VMEM((128, 1024), F32),
+            pltpu.VMEM((64, 1024), F32),
             pltpu.VMEM((128, 1024), F32),
             *constants,
             pltpu.VMEM((4, 4, 2, 128, 1024), BF16),
@@ -504,6 +543,8 @@
             pltpu.VMEM((16, 2, 768, 128), BF16),
             pltpu.VMEM((128, 1024), F32),
             pltpu.VMEM((128, 1024), F32),
+            pltpu.VMEM((128, 1024), F32),
+            pltpu.VMEM((4, 1024), F32),
             pltpu.VMEM((4, 32, 128), F32),
             pltpu.SemaphoreType.DMA((14,)),
             pltpu.SemaphoreType.DMA((16, 2)),
@@ -515,7 +556,7 @@
         ),
         cost_estimate=pl.CostEstimate(flops=13 * 10**9, bytes_accessed=20 * 10**6, transcendentals=0),
         name="gradients",
-    )(tokens, cotangent, weight, momentum, kept, rows, lanes, fold, tile_lane)
+    )(tokens, cotangent, weight, momentum, kept, rows, fold)
     return pl.pallas_call(
         last_kernel,
         out_shape=(
@@ -524,7 +565,7 @@
             jax.ShapeDtypeStruct((128, 1024), F32),
             jax.ShapeDtypeStruct((128, 1024), F32),
         ),
-        in_specs=[any_space] * 10,
+        in_specs=[any_space] * 8,
         out_specs=(any_space, any_space, any_space, any_space),
         scratch_shapes=[
             pltpu.VMEM((768, 4096), BF16),
@@ -539,7 +580,7 @@
         ],
         compiler_params=pltpu.CompilerParams(vmem_limit_bytes=60 << 20),
         name="step",
-    )(ig, newmom, shared, kept, weight, rows, lanes, fold, tile_lane, ones)
+    )(ig, newmom, shared, kept, weight, rows, fold, ones)
 
 
 def solution(mesh):

time: 85.9 us -> 81.5 us (0.949)
  Pallas kernels: 84.8 us -> 80.8 us
    pallas_call x1, Pallas kernels: 78.4 us -> 73.6 us  [body(): pl.pallas_call(main_kernel, out_shape=(jax.ShapeDtypeStruct((768, 4096),...]
where the time goes in v3:
time: 81.5 us; the launch traced here: 81.4 us
  Pallas kernels  80.8 us (99%)
    pallas_call x1, Pallas kernels, body(): pl.pallas_call(main_kernel, out_shape=(jax.ShapeDtypeStruct((768, 4096),...  73.6 us
    pallas_call x1, Pallas kernels, body(): pl.pallas_call(last_kernel, out_shape=(jax.ShapeDtypeStruct((768, 4096),...  7.16 us

profile of v3, /device:TPU:1, one launch (start us, length us, event | category | flops | bytes accessed | tf_op | source)
XLA Modules:
  0.0 81.4 jit_solution(11991601828171736327)
XLA Ops:
  0.6 73.6 %gradients.1 = (bf16[768,4096]{1,0:T(8,128)(2,1)}, f32[1,128,1024]{2,1,0:T(8,128)}, f32[4,32,128]{2,1,0:T(8,128)}) custom-call(bf16[768,4096]{1,0:T(8,128)(2,1)} %tok_hbm.1, bf16[768,1024]{1,0:T(8,128)(2,1)} %cot_hbm.1, f32[128,1024]{1,0:T(8,128)} %w_hbm.3, f32[1,128,1024]{2,1,0:T(8,128)} %mom_hbm.1, s32[4,4,16]{2,1,0:T(4,128)} %bitcast.3, ...), custom_call_target="tpu_custom_call" | custom-call | flops 12999999488 | bytes 20000000 | tf_op jit(solution)/shard_map/gradients/pallas_call | solution.py:520
  74.3 7.2 %step.1 = (bf16[768,4096]{1,0:T(8,128)(2,1)}, f32[1,128,1024]{2,1,0:T(8,128)}, f32[128,1024]{1,0:T(8,128)}, f32[128,1024]{1,0:T(8,128)}) custom-call(bf16[768,4096]{1,0:T(8,128)(2,1)} %get-tuple-element.7.ig_in, f32[1,128,1024]{2,1,0:T(8,128)} %get-tuple-element.8.mom_in, f32[4,32,128]{2,1,0:T(8,128)} %get-tuple-element.9.ex_hbm, s32[4,4,16]{2,1,0:T(4,128)} %bitcast.4, ...), custom_call_target="tpu_custom_call" | custom-call | tf_op jit(solution)/shard_map/step/pallas_call | solution.py:560

commit v4 on v3

--- a/solution.py
+++ b/solution.py
@@ -127,10 +127,10 @@
 
 def main_kernel(
     tok_hbm, cot_hbm, w_hbm, mom_hbm, kept_hbm, rows_hbm, fold_hbm,
-    ig_hbm, newmom_hbm, ex_hbm,
+    ig, newmom, ex_out,
     tok, cot, w, mom, kept_ref, rows_ref, fold_ref,
     wf, parts, got_y, got_s1, got_x2, got_z2, got_y2, got_last,
-    ig, cur, newmom, dense, numbers, ex, local_sem, ig_sem, send_sem, recv_sem,
+    cur, dense, numbers, ex, local_sem, send_sem, recv_sem,
 ):
     yhi, core, x, z, ylo, at = make_places()
     oy = 1 - ylo
@@ -334,16 +334,14 @@
             kept_here = jnp.where(masks[0][a] | masks[1][a], coefs[a], 0.0)
             dense[a * 64 : a * 64 + 64, cols] = kept_here.reshape(64, WIDTH)
 
-    def input_grad(plane, base, low, high):
+    def input_grad(plane, low, high):
         def one(i, carry):
             xx, zz = i // 2, (i % 2) * 2
             rows = jnp.concatenate([wf[xx, zz, plane], wf[xx, zz + 1, plane]], axis=0)
             out = lax.dot_general(cot[...], rows, TURNED, preferred_element_type=F32).astype(BF16)
-            ig[base + i, 0] = out[:, :128]
-            ig[base + i, 1] = out[:, 128:]
             for j in range(2):
                 cols = pl.ds(pl.multiple_of(((xx * 4 + zz + j) * 2 + plane) * 128, 128), 128)
-                pltpu.make_async_copy(ig.at[base + i, j], ig_hbm.at[:, cols], ig_sem.at[base + i, j]).start()
+                ig[:, cols] = out[:, j * 128 : j * 128 + 128]
             return carry
 
         lax.fori_loop(low, high, one, 0)
@@ -370,7 +368,7 @@
     far.append((same(wf.at[xk[0], :, ylo, rows_z], y_peer, "far"), wf.at[xk[0], :, oy, rows_z]))
     near = same(wf.at[:, :, ylo, rows_c], core_peer, "near")
     near.wait_recv()
-    input_grad(ylo, 0, 0, 8)
+    input_grad(ylo, 0, 8)
     pass_on(3)
     pass_on(6)
 
@@ -420,7 +418,7 @@
     finish_y(7)
     for copy in near2:
         copy.wait_recv()
-    input_grad(oy, 8, 0, 4)
+    input_grad(oy, 0, 4)
     finish(3)
     finish(6)
     finish(0)
@@ -428,49 +426,26 @@
     finish(4)
     finish(7)
     shared = [same(ex.at[me], peer, "ex") for peer in rep_peers]
-    newmom[...] = cur[...] - from_coefs(dense[...], rows_ref[...])
-    newmom_store = pltpu.make_async_copy(newmom, newmom_hbm.at[0], local_sem.at[12])
-    newmom_store.start()
-
-    input_grad(oy, 8, 4, 8)
+    newmom[0] = cur[...] - from_coefs(dense[...], rows_ref[...])
+
+    input_grad(oy, 4, 8)
     for copy in shared:
         copy.wait_recv()
-    ex_store = pltpu.make_async_copy(ex, ex_hbm, local_sem.at[13])
-    ex_store.start()
+    ex_out[...] = ex[...]
     for copy in sent:
         copy.wait_send()
 
-    def drain(i, carry):
-        for j in range(2):
-            pltpu.make_async_copy(ig.at[i, j], ig_hbm.at[:, pl.ds(0, 128)], ig_sem.at[i, j]).wait()
-        return carry
-
-    lax.fori_loop(0, 16, drain, 0)
-    newmom_store.wait()
-    ex_store.wait()
-
 
 def last_kernel(
-    ig_in, mom_in, ex_hbm, kept_hbm, w_hbm, rows_hbm, fold_hbm, ones_hbm,
-    ig_out, mom_out, neww_out, upd_out,
-    ig, mom, ex_ref, w_ref, kept_ref, rows_ref, fold_ref, ones_ref,
-    neww_ref, upd_ref, sem,
+    ig, mom, ex_ref, kept_ref, w_ref, rows_ref, fold_ref, ones_ref,
+    ig_out, mom_out, neww_out, upd_out, neww_ref, upd_ref, sem,
 ):
-    small = [
-        (ex_hbm, ex_ref), (kept_hbm, kept_ref), (fold_hbm, fold_ref), (rows_hbm, rows_ref), (ones_hbm, ones_ref),
-        (w_hbm, w_ref),
+    stores = [
+        pltpu.make_async_copy(ig.at[pl.ds(i * 192, 192)], ig_out.at[pl.ds(i * 192, 192)], sem.at[i]) for i in range(4)
     ]
-    small = [pltpu.make_async_copy(src, dst, sem.at[2, i]) for i, (src, dst) in enumerate(small)]
-    for load in small:
-        load.start()
-    pieces = [(ig_in.at[pl.ds(i * 96, 96)], ig.at[pl.ds(i * 96, 96)], ig_out.at[pl.ds(i * 96, 96)]) for i in range(8)]
-    pieces.append((mom_in, mom, mom_out))
-    loads = [pltpu.make_async_copy(src, mid, sem.at[0, i]) for i, (src, mid, _) in enumerate(pieces)]
-    stores = [pltpu.make_async_copy(mid, dst, sem.at[1, i]) for i, (_, mid, dst) in enumerate(pieces)]
-    for load in loads:
-        load.start()
-    for load in small:
-        load.wait()
+    stores.append(pltpu.make_async_copy(mom, mom_out, sem.at[4]))
+    for store in stores:
+        store.start()
     total = [jnp.zeros((8, 8, 1024), F32)] * 2
     wide = dot_marks(ex_ref[...].reshape(128, 128), fold_ref[...], TURNED).reshape(4, 2, 2, 8, 1024)
     numbers = kept_lanes(kept_ref[...].reshape(16, 16))
@@ -483,9 +458,6 @@
                 mask = places == jnp.broadcast_to(numbers[at : at + 1].reshape(1, 1, 1024), (8, 8, 1024))
                 value = jnp.where(mask, jnp.broadcast_to(wide[r, which, a][None], (8, 8, 1024)), value)
             total[a] += value
-        for load, store in list(zip(loads, stores))[2 * r : 2 * r + 2 + r // 3]:
-            load.wait()
-            store.start()
     field = jnp.concatenate([t.reshape(64, 1024) for t in total], axis=0)
     average = from_coefs(field, rows_ref[...]) * 0.25
     squares = jnp.sum((average * average).reshape(2, 64, 1024), axis=1)
@@ -499,7 +471,7 @@
             upd_ref[rows_a, cols] = update
             neww_ref[rows_a, cols] = w_ref[rows_a, cols] - STEP * update
     results = [(neww_ref, neww_out), (upd_ref, upd_out)]
-    results = [pltpu.make_async_copy(src, dst, sem.at[1, 9 + i]) for i, (src, dst) in enumerate(results)]
+    results = [pltpu.make_async_copy(src, dst, sem.at[5 + i]) for i, (src, dst) in enumerate(results)]
     for store in results:
         store.start()
     for store in stores + results:
@@ -507,6 +479,7 @@
 
 
 def body(tokens, cotangent, weight, momentum, kept):
+    vmem = pl.BlockSpec(memory_space=pltpu.VMEM)
     any_space = pl.BlockSpec(memory_space=pl.ANY)
     rows, fold = jnp.asarray(two_halves(dct_matrix(2))), jnp.asarray(fold_matrix())
     ones = jnp.asarray(np.kron(np.eye(2), np.ones((TILE, TILE))).astype(jnp.bfloat16))
@@ -517,15 +490,15 @@
         pltpu.VMEM((1024, 128), BF16),
     ]
     sems = 160
-    ig, newmom, shared = pl.pallas_call(
+    between = pl.pallas_call(
         main_kernel,
         out_shape=(
-            jax.ShapeDtypeStruct((768, 4096), BF16),
-            jax.ShapeDtypeStruct((1, 128, 1024), F32),
-            jax.ShapeDtypeStruct((4, 32, 128), F32),
+            pltpu.VMEM((768, 4096), BF16),
+            pltpu.VMEM((1, 128, 1024), F32),
+            pltpu.VMEM((4, 32, 128), F32),
         ),
         in_specs=[any_space] * 7,
-        out_specs=(any_space, any_space, any_space),
+        out_specs=(vmem, vmem, vmem),
         scratch_shapes=[
             pltpu.VMEM((768, 4096), BF16),
             pltpu.VMEM((768, 1024), BF16),
@@ -540,23 +513,21 @@
             pltpu.VMEM((3, 4, 128, WIDTH), BF16),
             pltpu.VMEM((6, 4, 128, WIDTH), BF16),
             pltpu.VMEM((8, 3, 128, WIDTH), BF16),
-            pltpu.VMEM((16, 2, 768, 128), BF16),
-            pltpu.VMEM((128, 1024), F32),
             pltpu.VMEM((128, 1024), F32),
             pltpu.VMEM((128, 1024), F32),
             pltpu.VMEM((4, 1024), F32),
             pltpu.VMEM((4, 32, 128), F32),
-            pltpu.SemaphoreType.DMA((14,)),
-            pltpu.SemaphoreType.DMA((16, 2)),
+            pltpu.SemaphoreType.DMA((10,)),
             pltpu.SemaphoreType.DMA((sems,)),
             pltpu.SemaphoreType.DMA((sems,)),
         ],
         compiler_params=pltpu.CompilerParams(
-            collective_id=0, has_side_effects=True, vmem_limit_bytes=60 << 20
+            collective_id=0, has_side_effects=True, vmem_limit_bytes=48 << 20
         ),
         cost_estimate=pl.CostEstimate(flops=13 * 10**9, bytes_accessed=20 * 10**6, transcendentals=0),
         name="gradients",
     )(tokens, cotangent, weight, momentum, kept, rows, fold)
+    between = [pltpu.with_memory_space_constraint(a, pltpu.VMEM) for a in between]
     return pl.pallas_call(
         last_kernel,
         out_shape=(
@@ -565,22 +536,16 @@
             jax.ShapeDtypeStruct((128, 1024), F32),
             jax.ShapeDtypeStruct((128, 1024), F32),
         ),
-        in_specs=[any_space] * 8,
+        in_specs=[vmem] * 8,
         out_specs=(any_space, any_space, any_space, any_space),
         scratch_shapes=[
-            pltpu.VMEM((768, 4096), BF16),
-            pltpu.VMEM((1, 128, 1024), F32),
-            pltpu.VMEM((4, 32, 128), F32),
-            pltpu.VMEM((128, 1024), F32),
-            *constants,
-            pltpu.VMEM((128, 128), BF16),
             pltpu.VMEM((128, 1024), F32),
             pltpu.VMEM((128, 1024), F32),
-            pltpu.SemaphoreType.DMA((3, 12)),
+            pltpu.SemaphoreType.DMA((7,)),
         ],
-        compiler_params=pltpu.CompilerParams(vmem_limit_bytes=60 << 20),
+        compiler_params=pltpu.CompilerParams(vmem_limit_bytes=40 << 20),
         name="step",
-    )(ig, newmom, shared, kept, weight, rows, fold, ones)
+    )(*between, kept, weight, rows, fold, ones)
 
 
 def solution(mesh):

time: 81.5 us -> 77.9 us (0.956)
  Pallas kernels: 80.8 us -> 77 us
    pallas_call x1, Pallas kernels: 7.16 us -> 4 us  [body(): pl.pallas_call(last_kernel, out_shape=(jax.ShapeDtypeStruct((768, 4096),...]
where the time goes in v4:
time: 77.9 us; the launch traced here: 77.8 us
  Pallas kernels  77 us (99%)
    pallas_call x1, Pallas kernels, body(): pl.pallas_call(main_kernel, out_shape=(pltpu.VMEM((768, 4096), BF16), plt...  73 us
    pallas_call x1, Pallas kernels, body(): pl.pallas_call(last_kernel, out_shape=(jax.ShapeDtypeStruct((768, 4096),...  4 us

profile of v4, /device:TPU:1, one launch (start us, length us, event | category | flops | bytes accessed | tf_op | source)
XLA Modules:
  0.0 77.8 jit_solution(3670868074332191477)
XLA Ops:
  0.6 0.0 copy-start
  0.6 0.0 copy-start.1
  0.7 0.0 copy-start.2
  0.7 0.0 copy-start.3
  0.7 0.0 copy-start.4
  0.7 73.0 %gradients.1 = (bf16[768,4096]{1,0:T(8,128)(2,1)S(1)}, f32[1,128,1024]{2,1,0:T(8,128)S(1)}, f32[4,32,128]{2,1,0:T(8,128)S(1)}) custom-call(bf16[768,4096]{1,0:T(8,128)(2,1)} %tok_hbm.1, bf16[768,1024]{1,0:T(8,128)(2,1)} %cot_hbm.1, f32[128,1024]{1,0:T(8,128)} %w_ref.1, f32[1,128,1024]{2,1,0:T(8,128)} %mom_hbm.1, s32[4,4,16]{2,1,0:T(4,128)} %bitcast.3, ...), custom_call_target="tpu_custom_call" | custom-call | flops 12999999488 | bytes 20000000 | tf_op jit(solution)/shard_map/gradients/pallas_call | solution.py:493
  73.7 0.0 copy-done
  73.8 0.0 copy-done.1
  73.8 0.0 copy-done.2
  73.8 0.0 copy-done.3
  73.8 0.0 copy-done.4
  73.8 4.0 %step.1 = (bf16[768,4096]{1,0:T(8,128)(2,1)}, f32[1,128,1024]{2,1,0:T(8,128)}, f32[128,1024]{1,0:T(8,128)}, f32[128,1024]{1,0:T(8,128)}) custom-call(bf16[768,4096]{1,0:T(8,128)(2,1)S(1)} %get-tuple-element.7.ig, f32[1,128,1024]{2,1,0:T(8,128)S(1)} %get-tuple-element.8.mom, f32[4,32,128]{2,1,0:T(8,128)S(1)} %get-tuple-element.9.ex_ref, ...), custom_call_target="tpu_custom_call" | custom-call | tf_op jit(solution)/shard_map/step/pallas_call | solution.py:531
Async XLA Ops:
  0.6 73.1 %copy-start = (f32[128,1024]{1,0:T(8,128)S(1)}, f32[128,1024]{1,0:T(8,128)}, u32[]{:S(2)}) copy-start(f32[128,1024]{1,0:T(8,128)} %w_ref.1) | copy-start | bytes 1572868
  0.6 73.1 %copy-start.1 = (bf16[1024,128]{1,0:T(8,128)(2,1)S(1)}, bf16[1024,128]{1,0:T(8,128)(2,1)}, u32[]{:S(2)}) copy-start(bf16[1024,128]{1,0:T(8,128)(2,1)} %constant.7.clone.fold_hbm.fold_ref) | copy-start | bytes 786436
  0.7 73.1 %copy-start.2 = (bf16[2,128,128]{2,1,0:T(8,128)(2,1)S(1)}, bf16[2,128,128]{2,1,0:T(8,128)(2,1)}, u32[]{:S(2)}) copy-start(bf16[2,128,128]{2,1,0:T(8,128)(2,1)} %constant.6.clone.rows_hbm.rows_ref) | copy-start | bytes 196612
  0.7 73.1 %copy-start.3 = (bf16[128,128]{1,0:T(8,128)(2,1)S(1)}, bf16[128,128]{1,0:T(8,128)(2,1)}, u32[]{:S(2)}) copy-start(bf16[128,128]{1,0:T(8,128)(2,1)} %constant.8.clone.ones_ref) | copy-start | bytes 98308
  0.7 73.1 %copy-start.4 = (s32[4,2,16,2]{2,3,1,0:T(2,128)S(1)}, s32[4,2,16,2]{2,3,1,0:T(2,128)}, u32[]{:S(2)}) copy-start(s32[4,2,16,2]{2,3,1,0:T(2,128)} %param.12) | copy-start | bytes 3076

commit v5 on v4

--- a/solution.py
+++ b/solution.py
@@ -199,16 +199,17 @@
         tok_loads[k].wait()
 
         def block(zz, carry, xs=xs):
-            cols = pl.ds(pl.multiple_of((xs * 4 + zz) * 256, 256), 256)
+            cols = pl.ds(pl.multiple_of((xs * 4 + zz * 2) * 256, 512), 512)
             part = lax.dot_general(
                 tok[:, cols], cot[...], FROM_LEFT, preferred_element_type=F32
             ).astype(BF16)
             for p in range(8):
-                parts[p, xs, zz, 0] = part[:128, p * WIDTH : p * WIDTH + WIDTH]
-                parts[p, xs, zz, 1] = part[128:, p * WIDTH : p * WIDTH + WIDTH]
+                for q in range(4):
+                    chunk = part[q * 128 : q * 128 + 128, p * WIDTH : p * WIDTH + WIDTH]
+                    parts[p, xs, zz * 2 + q // 2, q % 2] = chunk
             return carry
 
-        lax.fori_loop(0, 4, block, 0)
+        lax.fori_loop(0, 2, block, 0)
         y1.append([send(parts.at[p, xs, :, oy], got_y.at[p, xs], y_peer) for p in Y_PIECES])
         if k == 0:
             for copy in gx + gz:
@@ -307,32 +308,41 @@
         numbers[...] = kept_lanes(kept_ref[me])
         ex[me] = jnp.zeros((32, 128), F32)
 
-    def finish(p):
-        for copy in last[p]:
-            copy.wait_recv()
-        total = parts[p, x, z, ylo].astype(F32)
-        for k in range(3):
-            total += got_last[p, k].astype(F32)
-        cols = slice(p * WIDTH, p * WIDTH + WIDTH)
-        current = DECAY * mom[:, cols] + total * (1.0 / np.sqrt(24576.0))
-        cur[:, cols] = current
-        mid = dot_left(rows_ref[...], current)
-        coefs = dot_right(mid, rows_ref[...], TURNED).reshape(2, 8, 8, WIDTH)
+    def finish(*pieces):
+        fields = []
+        for p in pieces:
+            for copy in last[p]:
+                copy.wait_recv()
+            total = parts[p, x, z, ylo].astype(F32)
+            for k in range(3):
+                total += got_last[p, k].astype(F32)
+            cols = slice(p * WIDTH, p * WIDTH + WIDTH)
+            current = DECAY * mom[:, cols] + total * (1.0 / np.sqrt(24576.0))
+            cur[:, cols] = current
+            fields.append(current)
+        mid = dot_left(rows_ref[...], jnp.concatenate(fields, axis=1))
+        mid = jnp.concatenate([mid[:, i * WIDTH : i * WIDTH + WIDTH] for i in range(len(pieces))], axis=0)
+        coefs_all = dot_right(mid, rows_ref[...], TURNED)
         places = block_numbers(WIDTH)
-        masks = [
-            [
-                places == jnp.broadcast_to(numbers[2 * a + which, cols].reshape(1, 1, WIDTH), (8, 8, WIDTH))
-                for a in range(2)
+        shares = []
+        for i, p in enumerate(pieces):
+            coefs = coefs_all[i * 128 : i * 128 + 128].reshape(2, 8, 8, WIDTH)
+            cols = slice(p * WIDTH, p * WIDTH + WIDTH)
+            masks = [
+                [
+                    places == jnp.broadcast_to(numbers[2 * a + which, cols].reshape(1, 1, WIDTH), (8, 8, WIDTH))
+                    for a in range(2)
+                ]
+                for which in range(2)
             ]
-            for which in range(2)
-        ]
-        folded = [
-            jnp.sum(jnp.where(masks[which][a], coefs[a], 0.0), axis=0) for which in range(2) for a in range(2)
-        ]
-        ex[me] += dot_marks(jnp.concatenate(folded, axis=0), fold_ref[cols])
-        for a in range(2):
-            kept_here = jnp.where(masks[0][a] | masks[1][a], coefs[a], 0.0)
-            dense[a * 64 : a * 64 + 64, cols] = kept_here.reshape(64, WIDTH)
+            folded = [
+                jnp.sum(jnp.where(masks[which][a], coefs[a], 0.0), axis=0) for which in range(2) for a in range(2)
+            ]
+            shares.append(dot_marks(jnp.concatenate(folded, axis=0), fold_ref[cols]))
+            for a in range(2):
+                kept_here = jnp.where(masks[0][a] | masks[1][a], coefs[a], 0.0)
+                dense[a * 64 : a * 64 + 64, cols] = kept_here.reshape(64, WIDTH)
+        ex[me] += sum(shares[1:], shares[0])
 
     def input_grad(plane, low, high):
         def one(i, carry):
@@ -412,19 +422,15 @@
     finish_y(3)
     finish_y(6)
     forward(6)
-    finish(2)
-    finish(5)
+    finish(2, 5)
     finish_y(4)
     finish_y(7)
     for copy in near2:
         copy.wait_recv()
     input_grad(oy, 0, 4)
-    finish(3)
-    finish(6)
-    finish(0)
-    finish(1)
-    finish(4)
-    finish(7)
+    finish(3, 6)
+    finish(0, 1)
+    finish(4, 7)
     shared = [same(ex.at[me], peer, "ex") for peer in rep_peers]
     newmom[0] = cur[...] - from_coefs(dense[...], rows_ref[...])
 
@@ -437,15 +443,22 @@
 
 
 def last_kernel(
-    ig, mom, ex_ref, kept_ref, w_ref, rows_ref, fold_ref, ones_ref,
-    ig_out, mom_out, neww_out, upd_out, neww_ref, upd_ref, sem,
+    ig, mom, ex_ref, kept_hbm, w_hbm, rows_hbm, fold_hbm, ones_hbm,
+    ig_out, mom_out, neww_out, upd_out,
+    w_ref, kept_ref, rows_ref, fold_ref, ones_ref, neww_ref, upd_ref, sem,
 ):
+    small = [(kept_hbm, kept_ref), (fold_hbm, fold_ref), (rows_hbm, rows_ref), (ones_hbm, ones_ref), (w_hbm, w_ref)]
+    small = [pltpu.make_async_copy(src, dst, sem.at[7 + i]) for i, (src, dst) in enumerate(small)]
+    for load in small:
+        load.start()
     stores = [
         pltpu.make_async_copy(ig.at[pl.ds(i * 192, 192)], ig_out.at[pl.ds(i * 192, 192)], sem.at[i]) for i in range(4)
     ]
     stores.append(pltpu.make_async_copy(mom, mom_out, sem.at[4]))
     for store in stores:
         store.start()
+    for load in small:
+        load.wait()
     total = [jnp.zeros((8, 8, 1024), F32)] * 2
     wide = dot_marks(ex_ref[...].reshape(128, 128), fold_ref[...], TURNED).reshape(4, 2, 2, 8, 1024)
     numbers = kept_lanes(kept_ref[...].reshape(16, 16))
@@ -536,12 +549,15 @@
             jax.ShapeDtypeStruct((128, 1024), F32),
             jax.ShapeDtypeStruct((128, 1024), F32),
         ),
-        in_specs=[vmem] * 8,
+        in_specs=[vmem] * 3 + [any_space] * 5,
         out_specs=(any_space, any_space, any_space, any_space),
         scratch_shapes=[
             pltpu.VMEM((128, 1024), F32),
+            *constants,
+            pltpu.VMEM((128, 128), BF16),
             pltpu.VMEM((128, 1024), F32),
-            pltpu.SemaphoreType.DMA((7,)),
+            pltpu.VMEM((128, 1024), F32),
+            pltpu.SemaphoreType.DMA((12,)),
         ],
         compiler_params=pltpu.CompilerParams(vmem_limit_bytes=40 << 20),
         name="step",

time: 77.9 us -> 76.4 us (0.981)
  Pallas kernels: 77 us -> 75.5 us
    pallas_call x1, Pallas kernels: 73 us -> 72.1 us  [body(): pl.pallas_call(main_kernel, out_shape=(pltpu.VMEM((768, 4096), BF16), plt...]
where the time goes in v5:
time: 76.4 us; the launch traced here: 76.3 us
  Pallas kernels  75.5 us (99%)
    pallas_call x1, Pallas kernels, body(): pl.pallas_call(main_kernel, out_shape=(pltpu.VMEM((768, 4096), BF16), plt...  72.1 us
    pallas_call x1, Pallas kernels, body(): pl.pallas_call(last_kernel, out_shape=(jax.ShapeDtypeStruct((768, 4096),...  3.43 us

profile of v5, /device:TPU:1, one launch (start us, length us, event | category | flops | bytes accessed | tf_op | source)
XLA Modules:
  0.0 76.3 jit_solution(8405085698263193393)
XLA Ops:
  0.6 0.0 copy-start
  0.6 0.0 copy-start.1
  0.7 0.0 copy-start.2
  0.7 0.0 copy-start.3
  0.7 0.0 copy-start.4
  0.7 72.1 %gradients.1 = (bf16[768,4096]{1,0:T(8,128)(2,1)S(1)}, f32[1,128,1024]{2,1,0:T(8,128)S(1)}, f32[4,32,128]{2,1,0:T(8,128)S(1)}) custom-call(bf16[768,4096]{1,0:T(8,128)(2,1)} %tok_hbm.1, bf16[768,1024]{1,0:T(8,128)(2,1)} %cot_hbm.1, f32[128,1024]{1,0:T(8,128)} %w_hbm.3, f32[1,128,1024]{2,1,0:T(8,128)} %mom_hbm.1, s32[4,4,16]{2,1,0:T(4,128)} %bitcast.3, ...), custom_call_target="tpu_custom_call" | custom-call | flops 12999999488 | bytes 20000000 | tf_op jit(solution)/shard_map/gradients/pallas_call | solution.py:506
  72.8 0.0 copy-done
  72.8 0.0 copy-done.1
  72.8 0.0 copy-done.2
  72.8 0.0 copy-done.3
  72.8 0.0 copy-done.4
  72.8 3.4 %step.1 = (bf16[768,4096]{1,0:T(8,128)(2,1)}, f32[1,128,1024]{2,1,0:T(8,128)}, f32[128,1024]{1,0:T(8,128)}, f32[128,1024]{1,0:T(8,128)}) custom-call(bf16[768,4096]{1,0:T(8,128)(2,1)S(1)} %get-tuple-element.7.ig, f32[1,128,1024]{2,1,0:T(8,128)S(1)} %get-tuple-element.8.mom, f32[4,32,128]{2,1,0:T(8,128)S(1)} %get-tuple-element.9.ex_ref, ...), custom_call_target="tpu_custom_call" | custom-call | tf_op jit(solution)/shard_map/step/pallas_call | solution.py:544
Async XLA Ops:
  0.6 72.2 %copy-start = (f32[128,1024]{1,0:T(8,128)S(1)}, f32[128,1024]{1,0:T(8,128)}, u32[]{:S(2)}) copy-start(f32[128,1024]{1,0:T(8,128)} %w_hbm.3) | copy-start | bytes 1572868
  0.6 72.2 %copy-start.1 = (bf16[1024,128]{1,0:T(8,128)(2,1)S(1)}, bf16[1024,128]{1,0:T(8,128)(2,1)}, u32[]{:S(2)}) copy-start(bf16[1024,128]{1,0:T(8,128)(2,1)} %constant.7.clone.fold_hbm) | copy-start | bytes 786436
  0.7 72.2 %copy-start.2 = (bf16[2,128,128]{2,1,0:T(8,128)(2,1)S(1)}, bf16[2,128,128]{2,1,0:T(8,128)(2,1)}, u32[]{:S(2)}) copy-start(bf16[2,128,128]{2,1,0:T(8,128)(2,1)} %constant.6.clone.rows_hbm) | copy-start | bytes 196612
  0.7 72.2 %copy-start.3 = (bf16[128,128]{1,0:T(8,128)(2,1)S(1)}, bf16[128,128]{1,0:T(8,128)(2,1)}, u32[]{:S(2)}) copy-start(bf16[128,128]{1,0:T(8,128)(2,1)} %constant.8.clone.ones_hbm) | copy-start | bytes 98308
  0.7 72.2 %copy-start.4 = (s32[4,2,16,2]{2,3,1,0:T(2,128)S(1)}, s32[4,2,16,2]{2,3,1,0:T(2,128)}, u32[]{:S(2)}) copy-start(s32[4,2,16,2]{2,3,1,0:T(2,128)} %param.12) | copy-start | bytes 3076

commit v6 on v5

--- a/solution.py
+++ b/solution.py
@@ -251,7 +251,7 @@
             ref(i)[...] = total.astype(BF16)
             return carry
 
-        lax.fori_loop(0, count, one, 0)
+        lax.fori_loop(0, count, one, 0, unroll=min(2, count))
 
     def chunk_of(p, place, h):
         if p in X_PIECES:
@@ -377,10 +377,10 @@
     far.append((same(wf.at[:, zk[0], ylo, rows_x], y_far, "far"), wf.at[:, zk[0], oy, rows_x]))
     far.append((same(wf.at[xk[0], :, ylo, rows_z], y_peer, "far"), wf.at[xk[0], :, oy, rows_z]))
     near = same(wf.at[:, :, ylo, rows_c], core_peer, "near")
+    pass_on(3)
+    pass_on(6)
     near.wait_recv()
     input_grad(ylo, 0, 8)
-    pass_on(3)
-    pass_on(6)
 
     prepare()
     for k in range(4):

time: 76.4 us -> 76.3 us (level)
  no operation moved by 1% of the time
where the time goes in v6:
time: 76.3 us; the launch traced here: 76.2 us
  Pallas kernels  75.5 us (99%)
    pallas_call x1, Pallas kernels, body(): pl.pallas_call(main_kernel, out_shape=(pltpu.VMEM((768, 4096), BF16), plt...  72.1 us
    pallas_call x1, Pallas kernels, body(): pl.pallas_call(last_kernel, out_shape=(jax.ShapeDtypeStruct((768, 4096),...  3.43 us

profile of v6, /device:TPU:1, one launch (start us, length us, event | category | flops | bytes accessed | tf_op | source)
XLA Modules:
  0.0 76.2 jit_solution(8828928712943513288)
XLA Ops:
  0.6 0.0 copy-start
  0.6 0.0 copy-start.1
  0.7 0.0 copy-start.2
  0.7 0.0 copy-start.3
  0.7 0.0 copy-start.4
  0.7 72.1 %gradients.1 = (bf16[768,4096]{1,0:T(8,128)(2,1)S(1)}, f32[1,128,1024]{2,1,0:T(8,128)S(1)}, f32[4,32,128]{2,1,0:T(8,128)S(1)}) custom-call(bf16[768,4096]{1,0:T(8,128)(2,1)} %tok_hbm.1, bf16[768,1024]{1,0:T(8,128)(2,1)} %cot_hbm.1, f32[128,1024]{1,0:T(8,128)} %w_hbm.3, f32[1,128,1024]{2,1,0:T(8,128)} %mom_hbm.1, s32[4,4,16]{2,1,0:T(4,128)} %bitcast.3, ...), custom_call_target="tpu_custom_call" | custom-call | flops 12999999488 | bytes 20000000 | tf_op jit(solution)/shard_map/gradients/pallas_call | solution.py:506
  72.8 0.0 copy-done
  72.8 0.0 copy-done.1
  72.8 0.0 copy-done.2
  72.8 0.0 copy-done.3
  72.8 0.0 copy-done.4
  72.8 3.4 %step.1 = (bf16[768,4096]{1,0:T(8,128)(2,1)}, f32[1,128,1024]{2,1,0:T(8,128)}, f32[128,1024]{1,0:T(8,128)}, f32[128,1024]{1,0:T(8,128)}) custom-call(bf16[768,4096]{1,0:T(8,128)(2,1)S(1)} %get-tuple-element.7.ig, f32[1,128,1024]{2,1,0:T(8,128)S(1)} %get-tuple-element.8.mom, f32[4,32,128]{2,1,0:T(8,128)S(1)} %get-tuple-element.9.ex_ref, ...), custom_call_target="tpu_custom_call" | custom-call | tf_op jit(solution)/shard_map/step/pallas_call | solution.py:544
Async XLA Ops:
  0.6 72.1 %copy-start = (f32[128,1024]{1,0:T(8,128)S(1)}, f32[128,1024]{1,0:T(8,128)}, u32[]{:S(2)}) copy-start(f32[128,1024]{1,0:T(8,128)} %w_hbm.3) | copy-start | bytes 1572868
  0.6 72.1 %copy-start.1 = (bf16[1024,128]{1,0:T(8,128)(2,1)S(1)}, bf16[1024,128]{1,0:T(8,128)(2,1)}, u32[]{:S(2)}) copy-start(bf16[1024,128]{1,0:T(8,128)(2,1)} %constant.7.clone.fold_hbm) | copy-start | bytes 786436
  0.7 72.1 %copy-start.2 = (bf16[2,128,128]{2,1,0:T(8,128)(2,1)S(1)}, bf16[2,128,128]{2,1,0:T(8,128)(2,1)}, u32[]{:S(2)}) copy-start(bf16[2,128,128]{2,1,0:T(8,128)(2,1)} %constant.6.clone.rows_hbm) | copy-start | bytes 196612
  0.7 72.1 %copy-start.3 = (bf16[128,128]{1,0:T(8,128)(2,1)S(1)}, bf16[128,128]{1,0:T(8,128)(2,1)}, u32[]{:S(2)}) copy-start(bf16[128,128]{1,0:T(8,128)(2,1)} %constant.8.clone.ones_hbm) | copy-start | bytes 98308
  0.7 72.1 %copy-start.4 = (s32[4,2,16,2]{2,3,1,0:T(2,128)S(1)}, s32[4,2,16,2]{2,3,1,0:T(2,128)}, u32[]{:S(2)}) copy-start(s32[4,2,16,2]{2,3,1,0:T(2,128)} %param.12) | copy-start | bytes 3076
